TPU v7x, 128 devices: a whole 4x4x4 slice. The times are simulated.
128 devices in a mesh: blk: 32 (over y_lo, z, x), rep: 4 (over y_hi, core).
Axes of the slice: x: 4, y: 4 (y_hi: 2, y_lo: 2; y = y_hi * 2 + y_lo), z: 4, core: 2. Of those that a mesh axis runs over, the one named last changes fastest.
Arguments:
- features: bfloat16 [65536, 256], P(('blk', 'rep')), may hold values from -6 to 6
- tiles: bfloat16 [32, 4, 32, 12, 128, 128], P('blk', 'rep'), may hold values from -0.1875 to 0.1875
- patch_horizontal_bands: int32 [32, 4, 32, 12], P('blk', 'rep'), may hold values from 0 to 15, as said below
- patch_vertical_bands: int32 [32, 4, 32, 12], P('blk', 'rep'), may hold values from 0 to 3
- active_patch_numbers: int32 [32, 4, 32], P('blk', 'rep'), may hold values from 1 to 12, as said below
- weight: bfloat16 [256, 256], replicated, may hold values from -0.375 to 0.375
- cotangent: bfloat16 [65536, 256], P(('blk', 'rep')), may hold values from -6 to 6
Outputs:
- output: bfloat16 [65536, 256], P(('blk', 'rep'))
- grad_weight: float32 [256, 256], replicated
- grad_input: float32 [65536, 256], P(('blk', 'rep'))
Inputs may be any that keep to these rules, and one draw needn't show every extreme that they name: Within the first active_patch_numbers entries of a list, the pairs (patch_horizontal_bands, patch_vertical_bands) are distinct. active_patch_numbers[g, r, g] is 12 for every g and r.
All inputs are finite; a program needn't handle non-finite values.
Results may differ from a plain program's by a relative error of at most 0.0057.
Values may be sent and summed in bfloat16 or wider, within the bound.
A program may use at most 64 MiB of HBM per device.

v0:
```python
import math

import jax
import jax.numpy as jnp
from jax import lax
from jax.sharding import PartitionSpec as P


def shifted(shard, axis, by):
    devices = lax.axis_size(axis)
    return lax.ppermute(shard, axis, [(i, (i + by) % devices) for i in range(devices)])


def forward_terms(
    panel,
    tiles,
    patch_horizontal_bands,
    patch_vertical_bands,
    active_patch_numbers,
    source,
    group_blocks,
):
    block_tiles = lax.dynamic_index_in_dim(tiles, source, 0, keepdims=False)
    block_rows = lax.dynamic_index_in_dim(patch_horizontal_bands, source, 0, keepdims=False)
    block_cols = lax.dynamic_index_in_dim(patch_vertical_bands, source, 0, keepdims=False)
    active_patch_number = lax.dynamic_index_in_dim(active_patch_numbers, source, 0, keepdims=False)
    patch_limit = block_tiles.shape[0]
    block_size = block_tiles.shape[1]
    features_in = panel.reshape(-1, block_size, panel.shape[1])
    chosen = jnp.take(features_in, block_cols, axis=0)
    product = jnp.einsum("kij,kjf->kif", block_tiles, chosen, preferred_element_type=jnp.float32)
    patch_activity_mask = (jnp.arange(patch_limit, dtype=jnp.int32) < active_patch_number).astype(
        jnp.float32
    )
    patch_arrangement = (
        block_rows[None, :] == jnp.arange(group_blocks, dtype=jnp.int32)[:, None]
    ).astype(jnp.float32) * patch_activity_mask[None, :]
    return jnp.einsum("gk,kif->gif", patch_arrangement, product, precision=lax.Precision.HIGHEST)


def backward_terms(
    back_group,
    tiles,
    patch_horizontal_bands,
    patch_vertical_bands,
    active_patch_numbers,
    destination_submatrix,
    panel_blocks,
):
    block_tiles = lax.dynamic_index_in_dim(tiles, destination_submatrix, 0, keepdims=False)
    block_rows = lax.dynamic_index_in_dim(
        patch_horizontal_bands, destination_submatrix, 0, keepdims=False
    )
    block_cols = lax.dynamic_index_in_dim(
        patch_vertical_bands, destination_submatrix, 0, keepdims=False
    )
    active_patch_number = lax.dynamic_index_in_dim(
        active_patch_numbers, destination_submatrix, 0, keepdims=False
    )
    patch_limit = block_tiles.shape[0]
    chosen = jnp.take(back_group, block_rows, axis=0)
    product = jnp.einsum("kji,kjf->kif", block_tiles, chosen, preferred_element_type=jnp.float32)
    patch_activity_mask = (jnp.arange(patch_limit, dtype=jnp.int32) < active_patch_number).astype(
        jnp.float32
    )
    patch_arrangement = (
        block_cols[None, :] == jnp.arange(panel_blocks, dtype=jnp.int32)[:, None]
    ).astype(jnp.float32) * patch_activity_mask[None, :]
    return jnp.einsum("ck,kif->cif", patch_arrangement, product, precision=lax.Precision.HIGHEST)


def local(
    features,
    tiles,
    patch_horizontal_bands,
    patch_vertical_bands,
    active_patch_numbers,
    weight,
    cotangent,
):
    cycle_size = lax.axis_size("blk")
    replicas = lax.axis_size("rep")
    position = lax.axis_index("blk")
    own_tiles = tiles[0, 0]
    own_rows = patch_horizontal_bands[0, 0]
    own_cols = patch_vertical_bands[0, 0]
    own_counts = active_patch_numbers[0, 0]
    block_size = own_tiles.shape[2]
    feat_width = features.shape[1]
    panel_blocks = features.shape[0] // block_size
    group_blocks = panel_blocks * replicas

    def gather_terms(panel, source):
        return forward_terms(
            panel,
            own_tiles,
            own_rows,
            own_cols,
            own_counts,
            jnp.mod(source, cycle_size),
            group_blocks,
        )

    def forward_turn(step, carry):
        panel, partial_value = carry
        panel = shifted(panel, "blk", 1)
        return (panel, partial_value + gather_terms(panel, position - step))

    last_panel, partial_value = lax.fori_loop(
        1, cycle_size, forward_turn, (features, gather_terms(features, position))
    )
    partial_value = partial_value.reshape(group_blocks * block_size, feat_width)
    summed = lax.psum_scatter(partial_value, "rep", scatter_dimension=0, tiled=True)
    aggregated = summed.astype(jnp.bfloat16)
    linear = jnp.dot(aggregated, weight, preferred_element_type=jnp.float32)
    output = jax.nn.silu(linear).astype(jnp.bfloat16)
    sigma = jax.nn.sigmoid(linear)
    grad_linear = (cotangent.astype(jnp.float32) * sigma * (1.0 + linear * (1.0 - sigma))).astype(
        jnp.bfloat16
    )
    local_weight = lax.dot_general(
        aggregated, grad_linear, (((0,), (0,)), ((), ())), preferred_element_type=jnp.float32
    )
    total_rows = features.shape[0] * cycle_size * replicas
    grad_weight = lax.psum(local_weight, ("blk", "rep")) * jnp.float32(1.0 / math.sqrt(total_rows))
    back = lax.dot_general(
        grad_linear, weight, (((1,), (1,)), ((), ())), preferred_element_type=jnp.float32
    ).astype(jnp.bfloat16)
    back_group = lax.all_gather(back, "rep", axis=0, tiled=True).reshape(
        group_blocks, block_size, feat_width
    )

    def spread_terms(destination_submatrix):
        return backward_terms(
            back_group,
            own_tiles,
            own_rows,
            own_cols,
            own_counts,
            jnp.mod(destination_submatrix, cycle_size),
            panel_blocks,
        )

    empty_sum = jnp.zeros((panel_blocks, block_size, feat_width), jnp.float32)

    def backward_turn(step, carry):
        carry = carry + spread_terms(position + 1 + step)
        return shifted(carry, "blk", -1)

    travelled = lax.fori_loop(0, cycle_size - 1, backward_turn, empty_sum)
    grad_blocks = travelled + spread_terms(position)
    grad_input = grad_blocks.reshape(panel_blocks * block_size, feat_width)
    return (output, grad_weight, grad_input)


def solution(mesh):
    placed = (
        P(("blk", "rep"), None),
        P("blk", "rep", None, None, None, None),
        P("blk", "rep", None, None),
        P("blk", "rep", None, None),
        P("blk", "rep", None),
        P(),
        P(("blk", "rep"), None),
    )
    return jax.shard_map(
        local,
        mesh=mesh,
        in_specs=placed,
        out_specs=(P(("blk", "rep"), None), P(), P(("blk", "rep"), None)),
        check_vma=False,
    )
```

profile of v0, /device:TPU:0, one launch (start us, length us, event | category | flops | bytes accessed | tf_op | source)
XLA Modules:
  0.0 1386.5 jit_solution(5011467933412857876)
XLA Ops:
  18.1 518.7 %while.32 = (s32[]{:T(128)}, bf16[512,256]{1,0:T(8,128)(2,1)S(1)}, f32[16,128,256]{2,0,1:T(8,128)S(1)}, s32[]{:T(128)}, s32[32,12]{1,0:T(8,128)S(1)}, /*index=5*...) while((s32[]{:T(128)}, bf16[512,256]{1,0:T(8,128)(2,1)S(1)}, ...), condition=%wide.region_1.3_spmd, body=%wide.region_0.2_spmd.sunk | while | flops 177079792 | bytes 11695536 | solution.py:109
  21.1 10.8 collective-permute-done
  38.7 10.4 collective-permute-done
  56.0 9.4 collective-permute-done
  88.4 9.3 collective-permute-done
  104.5 9.3 collective-permute-done
  152.8 9.3 collective-permute-done
  201.1 9.8 collective-permute-done
  217.8 11.0 collective-permute-done
  235.7 12.0 collective-permute-done
  254.5 11.1 collective-permute-done
  272.5 10.3 collective-permute-done
  289.6 9.4 collective-permute-done
  322.0 9.3 collective-permute-done
  338.1 9.3 collective-permute-done
  434.7 9.9 collective-permute-done
  451.5 11.1 collective-permute-done
  469.4 11.9 collective-permute-done
  488.2 11.0 collective-permute-done
  539.5 34.6 %reduce-scatter.2.cloned.1.call-done = f32[512,256]{1,0:T(8,128)} async-done(((f32[2048,256]{1,0:T(8,128)}), f32[512,256]{1,0:T(8,128)}) %reduce-scatter.2.cloned.1.call-update) | async-done | bytes 524304 | tf_op jit(solution)/shard_map/reduce_scatter | solution.py:113
  578.6 142.9 %all-reduce.2.cloned.1.call-done = f32[256,256]{1,0:T(8,128)} async-done(((f32[256,256]{1,0:T(8,128)}), f32[256,256]{1,0:T(8,128)}) %all-reduce.2.cloned.1.call-update) | async-done | bytes 262160 | tf_op jit(solution)/shard_map/psum | solution.py:125
  723.2 18.5 %all-gather.2.cloned.1.call-done = bf16[2048,256]{1,0:T(8,128)(2,1)} async-done(((bf16[512,256]{1,0:T(8,128)(2,1)}), bf16[2048,256]{1,0:T(8,128)(2,1)}) %all-gather.2.cloned.1.call-update) | async-done | bytes 1048592 | tf_op jit(solution)/shard_map/all_gather | solution.py:129
  746.3 629.3 %while.33 = (s32[]{:T(128)}, f32[4,128,256]{2,0,1:T(4,128)S(1)}, s32[]{:T(128)}, s32[32,12]{1,0:T(8,128)S(1)}, s32[32]{0:T(128)S(1)}, /*index=5*/bf16[32,12,128,...) while((s32[]{:T(128)}, f32[4,128,256]{2,0,1:T(4,128)S(1)}, ...), condition=%wide.region_5.8_spmd, body=%wide.region_4.7_spmd.sunk | while | flops 120063184 | bytes 9048860 | solution.py:150
  756.9 11.6 collective-permute-done.1
  780.6 10.8 collective-permute-done.1
  803.5 9.8 collective-permute-done.1
  1039.6 9.8 collective-permute-done.1
  1061.5 10.9 collective-permute-done.1
  1084.5 12.0 collective-permute-done.1
  1108.7 11.5 collective-permute-done.1
  1132.3 10.6 collective-permute-done.1
  1155.1 9.7 collective-permute-done.1
  (987 shorter events, 888.6 us)
Async XLA Ops:
  7.2 566.9 %reduce-scatter.2.cloned.1.call-start = ((), (), s32[]{:S(2)}) async-start(), calls=%async_computation.1 | async-start | bytes 2621440 | tf_op jit(solution)/shard_map/reduce_scatter | solution.py:113
  18.2 13.7 collective-permute-start
  539.4 182.1 %all-reduce.2.cloned.1.call-start = ((), (), s32[]{:S(2)}) async-start(), calls=%async_computation.2 | async-start | bytes 524288 | tf_op jit(solution)/shard_map/psum | solution.py:125
  577.3 164.4 %all-gather.2.cloned.1.call-start = ((), (), s32[]{:S(2)}) async-start(), calls=%async_computation.3 | async-start | bytes 1310720 | tf_op jit(solution)/shard_map/all_gather | solution.py:129
  751.7 16.7 %collective-permute-start.1 = (f32[4,128,256]{2,0,1:T(4,128)S(1)}, f32[4,128,256]{2,0,1:T(4,128)S(1)}, u32[]{:S(2)}, u32[]{:S(2)}) collective-permute-start(f32[4,128,256]{2,0,1:T(4,128)S(1)} %fusion.112), channel_id=1, source_target_pairs={{0,124},{4,0},{8,4},{12,8},{16,12},{20,16},{24,20},{28,24},{32,28}... | collective-permute-start | bytes 1572872 | tf_op jit(solution)/shard_map/while/body/eval_jaxpr/ppermute | solution.py:11
  773.9 17.5 %collective-permute-start.1 = (f32[4,128,256]{2,0,1:T(4,128)S(1)}, f32[4,128,256]{2,0,1:T(4,128)S(1)}, u32[]{:S(2)}, u32[]{:S(2)}) collective-permute-start(f32[4,128,256]{2,0,1:T(4,128)S(1)} %fusion.112), channel_id=1, source_target_pairs={{0,124},{4,0},{8,4},{12,8},{16,12},{20,16},{24,20},{28,24},{32,28}... | collective-permute-start | bytes 1572872 | tf_op jit(solution)/shard_map/while/body/eval_jaxpr/ppermute | solution.py:11
  796.8 16.6 %collective-permute-start.1 = (f32[4,128,256]{2,0,1:T(4,128)S(1)}, f32[4,128,256]{2,0,1:T(4,128)S(1)}, u32[]{:S(2)}, u32[]{:S(2)}) collective-permute-start(f32[4,128,256]{2,0,1:T(4,128)S(1)} %fusion.112), channel_id=1, source_target_pairs={{0,124},{4,0},{8,4},{12,8},{16,12},{20,16},{24,20},{28,24},{32,28}... | collective-permute-start | bytes 1572872 | tf_op jit(solution)/shard_map/while/body/eval_jaxpr/ppermute | solution.py:11
  818.8 15.7 %collective-permute-start.1 = (f32[4,128,256]{2,0,1:T(4,128)S(1)}, f32[4,128,256]{2,0,1:T(4,128)S(1)}, u32[]{:S(2)}, u32[]{:S(2)}) collective-permute-start(f32[4,128,256]{2,0,1:T(4,128)S(1)} %fusion.112), channel_id=1, source_target_pairs={{0,124},{4,0},{8,4},{12,8},{16,12},{20,16},{24,20},{28,24},{32,28}... | collective-permute-start | bytes 1572872 | tf_op jit(solution)/shard_map/while/body/eval_jaxpr/ppermute | solution.py:11
  839.8 14.8 %collective-permute-start.1 = (f32[4,128,256]{2,0,1:T(4,128)S(1)}, f32[4,128,256]{2,0,1:T(4,128)S(1)}, u32[]{:S(2)}, u32[]{:S(2)}) collective-permute-start(f32[4,128,256]{2,0,1:T(4,128)S(1)} %fusion.112), channel_id=1, source_target_pairs={{0,124},{4,0},{8,4},{12,8},{16,12},{20,16},{24,20},{28,24},{32,28}... | collective-permute-start | bytes 1572872 | tf_op jit(solution)/shard_map/while/body/eval_jaxpr/ppermute | solution.py:11
  860.0 13.8 collective-permute-start.1
  879.2 13.5 collective-permute-start.1
  898.0 13.5 collective-permute-start.1
  916.9 13.5 collective-permute-start.1
  954.6 13.5 collective-permute-start.1
  973.4 13.5 collective-permute-start.1
  992.3 14.4 %collective-permute-start.1 = (f32[4,128,256]{2,0,1:T(4,128)S(1)}, f32[4,128,256]{2,0,1:T(4,128)S(1)}, u32[]{:S(2)}, u32[]{:S(2)}) collective-permute-start(f32[4,128,256]{2,0,1:T(4,128)S(1)} %fusion.112), channel_id=1, source_target_pairs={{0,124},{4,0},{8,4},{12,8},{16,12},{20,16},{24,20},{28,24},{32,28}... | collective-permute-start | bytes 1572872 | tf_op jit(solution)/shard_map/while/body/eval_jaxpr/ppermute | solution.py:11
  1012.0 15.5 %collective-permute-start.1 = (f32[4,128,256]{2,0,1:T(4,128)S(1)}, f32[4,128,256]{2,0,1:T(4,128)S(1)}, u32[]{:S(2)}, u32[]{:S(2)}) collective-permute-start(f32[4,128,256]{2,0,1:T(4,128)S(1)} %fusion.112), channel_id=1, source_target_pairs={{0,124},{4,0},{8,4},{12,8},{16,12},{20,16},{24,20},{28,24},{32,28}... | collective-permute-start | bytes 1572872 | tf_op jit(solution)/shard_map/while/body/eval_jaxpr/ppermute | solution.py:11
  1032.9 16.5 %collective-permute-start.1 = (f32[4,128,256]{2,0,1:T(4,128)S(1)}, f32[4,128,256]{2,0,1:T(4,128)S(1)}, u32[]{:S(2)}, u32[]{:S(2)}) collective-permute-start(f32[4,128,256]{2,0,1:T(4,128)S(1)} %fusion.112), channel_id=1, source_target_pairs={{0,124},{4,0},{8,4},{12,8},{16,12},{20,16},{24,20},{28,24},{32,28}... | collective-permute-start | bytes 1572872 | tf_op jit(solution)/shard_map/while/body/eval_jaxpr/ppermute | solution.py:11
  1054.8 17.6 %collective-permute-start.1 = (f32[4,128,256]{2,0,1:T(4,128)S(1)}, f32[4,128,256]{2,0,1:T(4,128)S(1)}, u32[]{:S(2)}, u32[]{:S(2)}) collective-permute-start(f32[4,128,256]{2,0,1:T(4,128)S(1)} %fusion.112), channel_id=1, source_target_pairs={{0,124},{4,0},{8,4},{12,8},{16,12},{20,16},{24,20},{28,24},{32,28}... | collective-permute-start | bytes 1572872 | tf_op jit(solution)/shard_map/while/body/eval_jaxpr/ppermute | solution.py:11
  1077.8 18.8 %collective-permute-start.1 = (f32[4,128,256]{2,0,1:T(4,128)S(1)}, f32[4,128,256]{2,0,1:T(4,128)S(1)}, u32[]{:S(2)}, u32[]{:S(2)}) collective-permute-start(f32[4,128,256]{2,0,1:T(4,128)S(1)} %fusion.112), channel_id=1, source_target_pairs={{0,124},{4,0},{8,4},{12,8},{16,12},{20,16},{24,20},{28,24},{32,28}... | collective-permute-start | bytes 1572872 | tf_op jit(solution)/shard_map/while/body/eval_jaxpr/ppermute | solution.py:11
  1101.9 18.2 %collective-permute-start.1 = (f32[4,128,256]{2,0,1:T(4,128)S(1)}, f32[4,128,256]{2,0,1:T(4,128)S(1)}, u32[]{:S(2)}, u32[]{:S(2)}) collective-permute-start(f32[4,128,256]{2,0,1:T(4,128)S(1)} %fusion.112), channel_id=1, source_target_pairs={{0,124},{4,0},{8,4},{12,8},{16,12},{20,16},{24,20},{28,24},{32,28}... | collective-permute-start | bytes 1572872 | tf_op jit(solution)/shard_map/while/body/eval_jaxpr/ppermute | solution.py:11
  1125.6 17.4 %collective-permute-start.1 = (f32[4,128,256]{2,0,1:T(4,128)S(1)}, f32[4,128,256]{2,0,1:T(4,128)S(1)}, u32[]{:S(2)}, u32[]{:S(2)}) collective-permute-start(f32[4,128,256]{2,0,1:T(4,128)S(1)} %fusion.112), channel_id=1, source_target_pairs={{0,124},{4,0},{8,4},{12,8},{16,12},{20,16},{24,20},{28,24},{32,28}... | collective-permute-start | bytes 1572872 | tf_op jit(solution)/shard_map/while/body/eval_jaxpr/ppermute | solution.py:11
  1148.3 16.5 %collective-permute-start.1 = (f32[4,128,256]{2,0,1:T(4,128)S(1)}, f32[4,128,256]{2,0,1:T(4,128)S(1)}, u32[]{:S(2)}, u32[]{:S(2)}) collective-permute-start(f32[4,128,256]{2,0,1:T(4,128)S(1)} %fusion.112), channel_id=1, source_target_pairs={{0,124},{4,0},{8,4},{12,8},{16,12},{20,16},{24,20},{28,24},{32,28}... | collective-permute-start | bytes 1572872 | tf_op jit(solution)/shard_map/while/body/eval_jaxpr/ppermute | solution.py:11
  1170.2 15.6 %collective-permute-start.1 = (f32[4,128,256]{2,0,1:T(4,128)S(1)}, f32[4,128,256]{2,0,1:T(4,128)S(1)}, u32[]{:S(2)}, u32[]{:S(2)}) collective-permute-start(f32[4,128,256]{2,0,1:T(4,128)S(1)} %fusion.112), channel_id=1, source_target_pairs={{0,124},{4,0},{8,4},{12,8},{16,12},{20,16},{24,20},{28,24},{32,28}... | collective-permute-start | bytes 1572872 | tf_op jit(solution)/shard_map/while/body/eval_jaxpr/ppermute | solution.py:11
  1191.2 14.6 %collective-permute-start.1 = (f32[4,128,256]{2,0,1:T(4,128)S(1)}, f32[4,128,256]{2,0,1:T(4,128)S(1)}, u32[]{:S(2)}, u32[]{:S(2)}) collective-permute-start(f32[4,128,256]{2,0,1:T(4,128)S(1)} %fusion.112), channel_id=1, source_target_pairs={{0,124},{4,0},{8,4},{12,8},{16,12},{20,16},{24,20},{28,24},{32,28}... | collective-permute-start | bytes 1572872 | tf_op jit(solution)/shard_map/while/body/eval_jaxpr/ppermute | solution.py:11
  1211.2 13.7 collective-permute-start.1
  1230.3 13.5 collective-permute-start.1
  1249.1 13.5 collective-permute-start.1
  1305.6 13.5 collective-permute-start.1
  1324.5 13.5 collective-permute-start.1
  1343.3 13.5 collective-permute-start.1
  1362.2 13.5 collective-permute-start.1
  (199 other events, 2998.3 us)
Sparse Core Ops, SparseCore 0:
  539.5 34.4 reduce-scatter.1
  580.1 141.3 all-reduce.1
  723.8 17.8 all-gather.1
where the time goes:
time: 1390 us
  waiting for transfers between devices  755 us (54%)
  matrix products  267 us (19%)
  starting transfers between devices  212 us (15%)
  local copies, waits for them, and re-layouts  87.7 us (6%)
  other arithmetic  43 us (3%)
  between operations  13.9 us (1%)
    ppermute x62, waiting for transfers between devices, shifted(): lax.ppermute(shard, axis, [(i, (i + by) % devices) for i in range(devices)])  559 us
    ppermute x62, starting transfers between devices, shifted(): lax.ppermute(shard, axis, [(i, (i + by) % devices) for i in range(devices)])  212 us
    psum x1, waiting for transfers between devices, local(): lax.psum(local_weight, ('blk', 'rep'))  143 us
    dot_general x32, matrix products, forward_terms(): jnp.einsum('gk,kif->gif', patch_arrangement, product, precision=lax.Preci...  104 us
    dot_general x32, matrix products, backward_terms(): jnp.einsum('ck,kif->cif', patch_arrangement, product, precision=lax.Preci...  66.5 us
    dot_general x32, matrix products, backward_terms(): jnp.einsum('kji,kjf->kif', block_tiles, chosen, preferred_element_type=jn...  47 us
    dot_general x32, matrix products, forward_terms(): jnp.einsum('kij,kjf->kif', block_tiles, chosen, preferred_element_type=jn...  46.1 us
    reduce_scatter x1, waiting for transfers between devices, local(): lax.psum_scatter(partial_value, 'rep', scatter_dimension=0, tiled=True)  34.6 us
  transfers between devices with their start and end apart: 65, of which 65 were waited for; matrix products, arithmetic and copies ran while one was open for 3% of the time, Pallas kernels for 0%

commit v1 on v0

v1 whole, which is shorter than its diff:
```python
import functools
import math

import jax
import jax.numpy as jnp
from jax import lax
from jax.experimental import pallas as pl
from jax.experimental.pallas import tpu as pltpu
from jax.sharding import PartitionSpec as P

MESH = pl.DeviceIdType.MESH
F = 256
BS = 128
CAP = 12
PANELS = 32
PANEL = 512
HALF = 256
QUARTER = 128
SLOTS = PANELS * CAP
bf16 = jnp.bfloat16
f32 = jnp.float32


class Place:
    def __init__(self):
        b = lax.axis_index("blk")
        r = lax.axis_index("rep")
        self.b, self.r = b, r
        self.c = {"x": lax.rem(b, 4), "z": lax.rem(b // 4, 4)}
        self.y = b // 16
        self.yp = 1 - self.y
        self.core = lax.rem(r, 2)
        self.yh = r // 2
        self.nb = {"y": {"blk": self.blk(self.yp, self.c["z"], self.c["x"])}}
        for axis in ("x", "z"):
            for name, step in (("+", 1), ("-", -1), ("2", 2)):
                self.nb[axis + name] = {"blk": self.at(self.y, axis, step, 0)}
        self.nb["core"] = {"rep": self.yh * 2 + 1 - self.core}
        self.nb["yh"] = {"rep": (1 - self.yh) * 2 + self.core}

    def blk(self, y, z, x):
        return y * 16 + z * 4 + x

    def up(self, axis, step):
        return lax.rem(self.c[axis] + step + 4, 4)

    def at(self, y, first, d, e):
        if first == "x":
            return self.blk(y, self.up("z", e), self.up("x", d))
        return self.blk(y, self.up("z", d), self.up("x", e))

    def on_second(self, y, first, d, e):
        if first == "x":
            return self.blk(y, e, self.up("x", d))
        return self.blk(y, self.up("z", d), e)

    def barrier(self, names):
        sem = pltpu.get_barrier_semaphore()
        for name in names:
            pl.semaphore_signal(sem, inc=1, device_id=self.nb[name], device_id_type=MESH)
        pl.semaphore_wait(sem, len(names))


class Sends:
    def __init__(self, place, send, recv):
        self.place, self.send, self.recv = place, send, recv
        self.count = 0
        self.pending = []

    def to(self, where, src, dst):
        t = self.count
        self.count += 1
        copy = pltpu.make_async_remote_copy(
            src, dst, self.send.at[t], self.recv.at[t],
            device_id=self.place.nb[where], device_id_type=MESH,
        )
        copy.start()
        self.pending.append(copy)
        return t

    def wait(self, t, dst):
        pltpu.make_async_remote_copy(
            dst, dst, self.send.at[t], self.recv.at[t],
            device_id=self.place.nb["y"], device_id_type=MESH,
        ).wait_recv()

    def drain(self):
        for copy in self.pending:
            copy.wait_send()


PARTS = (("x", "z", 0), ("z", "x", 1))


def load_tiles(tiles_hbm, tiles, sem):
    copies = [
        pltpu.make_async_copy(
            tiles_hbm.at[pl.ds(i * SLOTS // 4, SLOTS // 4)],
            tiles.at[pl.ds(i * SLOTS // 4, SLOTS // 4)],
            sem.at[i],
        )
        for i in range(4)
    ]
    for copy in copies:
        copy.start()
    return copies


def forward_kernel(
    inv, f_ref, tiles_hbm, w_ref, ct_ref,
    out_ref, gw_ref, bt_ref,
    g, tiles, acc, in1, sbuf, in2, send, recv, loc,
):
    me = Place()
    names = ("x+", "x-", "z+", "z-", "y", "core", "yh")
    me.barrier(names)
    sends = Sends(me, send, recv)
    own = pltpu.make_async_copy(f_ref, g.at[me.b], loc.at[4])
    own.start()

    def rows(blk, lo, n):
        return g.at[blk, pl.ds(lo, n)]

    def push(where, blk, lo, n, mine=False):
        src = f_ref.at[pl.ds(lo, n)] if mine else rows(blk, lo, n)
        return sends.to(where, src, rows(blk, lo, n))

    def arrive(t, blk, lo, n):
        sends.wait(t, rows(blk, lo, n))

    to_y = [push("y", me.b, i * HALF, HALF, True) for i in range(2)]
    p1, p1f, p2, p2f = {}, {}, {}, {}

    def start2(y, s, p, d, mine=False):
        blk = me.at(y, p[0], d, 0)
        lo = p[2] * HALF
        p2[s, p[2], d] = (push(p[1] + "+", blk, lo, HALF, mine), push(p[1] + "-", blk, lo, HALF, mine))

    def stage1(y, s, mine):
        for p in PARTS:
            blk = me.at(y, p[0], 0, 0)
            lo = p[2] * HALF
            p1[s, p[2]] = (push(p[0] + "+", blk, lo, HALF, mine), push(p[0] + "-", blk, lo, HALF, mine))
        for p in PARTS:
            start2(y, s, p, 0, mine)

    def stage2(y, s):
        for p in PARTS:
            lo = p[2] * HALF
            t = p1[s, p[2]]
            arrive(t[0], me.at(y, p[0], -1, 0), lo, HALF)
            f0 = push(p[0] + "+", me.at(y, p[0], -1, 0), lo, QUARTER)
            start2(y, s, p, -1)
            arrive(t[1], me.at(y, p[0], 1, 0), lo, HALF)
            f1 = push(p[0] + "-", me.at(y, p[0], 1, 0), lo + QUARTER, QUARTER)
            start2(y, s, p, 1)
            p1f[s, p[2]] = (f0, f1)

    def stage3(y, s):
        for p in PARTS:
            lo = p[2] * HALF
            f0, f1 = p1f[s, p[2]]
            arrive(f0, me.at(y, p[0], 2, 0), lo, QUARTER)
            arrive(f1, me.at(y, p[0], 2, 0), lo + QUARTER, QUARTER)
            start2(y, s, p, 2)

    def stage4(y, s, d):
        for p in PARTS:
            lo = p[2] * HALF
            t = p2[s, p[2], d]
            arrive(t[0], me.at(y, p[0], d, -1), lo, HALF)
            f0 = push(p[1] + "+", me.at(y, p[0], d, -1), lo, QUARTER)
            arrive(t[1], me.at(y, p[0], d, 1), lo, HALF)
            f1 = push(p[1] + "-", me.at(y, p[0], d, 1), lo + QUARTER, QUARTER)
            p2f[s, p[2], d] = (f0, f1)

    def compute(y, p, d, first=False):
        lo = p[2] * HALF

        @pl.loop(0, 4)
        def _(hg):
            lhs = []
            for e in range(4):
                blk = me.on_second(y, p[0], d, e)
                for v in range(2):
                    base = blk * 64 + hg * 16 + p[2] * 2 + v
                    lhs.append(jnp.concatenate([tiles[inv[base + h * 4]] for h in range(4)], axis=0))
            lhs = jnp.concatenate(lhs, axis=1)
            rhs = jnp.concatenate(
                [g[me.on_second(y, p[0], d, e), pl.ds(lo, HALF), :] for e in range(4)], axis=0
            )
            part = jnp.dot(lhs, rhs, preferred_element_type=f32)
            if first:
                acc[hg] = part
            else:
                acc[hg] += part

    def stage5(y, s, d, first=False):
        for p in PARTS:
            lo = p[2] * HALF
            f0, f1 = p2f[s, p[2], d]
            arrive(f0, me.at(y, p[0], d, 2), lo, QUARTER)
            arrive(f1, me.at(y, p[0], d, 2), lo + QUARTER, QUARTER)
            compute(y, p, d, first and p[2] == 0)

    y, yp = me.y, me.yp
    stage1(y, 0, True)
    loads = load_tiles(tiles_hbm, tiles, loc)
    tiles[SLOTS] = jnp.zeros((BS, BS), bf16)
    twin = me.blk(yp, me.c["z"], me.c["x"])
    for i in range(2):
        arrive(to_y[i], twin, i * HALF, HALF)
    stage2(y, 0)
    stage1(yp, 1, False)
    stage3(y, 0)
    for d in (0, -1, 1):
        stage4(y, 0, d)
    stage2(yp, 1)
    stage4(y, 0, 2)
    stage3(yp, 1)
    own.wait()
    for copy in loads:
        copy.wait()
    stage5(y, 0, 0, True)
    stage4(yp, 1, 0)
    stage5(y, 0, -1)
    stage4(yp, 1, -1)
    stage5(y, 0, 1)
    stage4(yp, 1, 1)
    stage5(y, 0, 2)
    stage4(yp, 1, 2)
    for d in (0, -1, 1, 2):
        stage5(yp, 1, d)

    far = 1 - me.yh
    other = 1 - me.core
    t_far = sends.to("core", acc.at[far * 2 + other], in1.at[far])
    t_near = sends.to("core", acc.at[me.yh * 2 + other], in1.at[me.yh])
    sends.wait(t_far, in1.at[far])
    sbuf[...] = (acc[far * 2 + me.core] + in1[far]).astype(bf16)
    t_yh = sends.to("yh", sbuf, in2)
    sends.wait(t_near, in1.at[me.yh])
    near = acc[me.r] + in1[me.yh]
    acc[me.r] = near
    sends.wait(t_yh, in2)
    agg = (acc[me.r] + in2[...].astype(f32)).astype(bf16)
    linear = jnp.dot(agg, w_ref[...], preferred_element_type=f32)
    sigma = 1.0 / (1.0 + jnp.exp(-linear))
    out_ref[...] = (linear * sigma).astype(bf16)
    gl = (ct_ref[...].astype(f32) * sigma * (1.0 + linear * (1.0 - sigma))).astype(bf16)
    back = lax.dot_general(w_ref[...], gl, (((1,), (1,)), ((), ())), preferred_element_type=f32)
    bt_ref[me.r] = back.astype(bf16)
    b_yh = sends.to("yh", bt_ref.at[me.r], bt_ref.at[me.r])
    b_core = sends.to("core", bt_ref.at[me.r], bt_ref.at[me.r])
    gw_ref[...] = lax.dot_general(agg, gl, (((0,), (0,)), ((), ())), preferred_element_type=f32)
    there = far * 2 + me.core
    sends.wait(b_yh, bt_ref.at[there])
    b_fwd = sends.to("core", bt_ref.at[there], bt_ref.at[there])
    sends.wait(b_core, bt_ref.at[me.yh * 2 + other])
    sends.wait(b_fwd, bt_ref.at[far * 2 + other])
    sends.drain()
    assert sends.count <= 90


def backward_kernel(
    inv, tiles_hbm, bt_ref, gwp_ref,
    gi_ref, gw_ref,
    tiles, pbuf, in_h, in_f, sb, in_h1, in_f1, tb, sy, in_y,
    gx, gz, gb, gacc, send, recv, loc,
):
    me = Place()
    names = ("x+", "x-", "x2", "z+", "z-", "z2", "y", "core", "yh")
    me.barrier(names)
    sends = Sends(me, send, recv)
    loads = load_tiles(tiles_hbm, tiles, loc)
    tiles[SLOTS] = jnp.zeros((BS, BS), bf16)
    D = (2, -1, 1, 0)
    lo, hi = pl.ds(0, QUARTER), pl.ds(QUARTER, QUARTER)
    y, yp = me.y, me.yp
    ys = (y, yp)

    cx, cz = me.c["x"], me.c["z"]

    def piece(axis_x, n, ref):
        return ref.at[pl.ds(axis_x * n, n)]

    hops = ((1, "+"), (2, "2"), (3, "-"))
    t_gx = [
        sends.to("x" + name, piece(me.up("x", step), 64, gwp_ref), gx.at[i])
        for i, (step, name) in enumerate(hops)
    ]
    gstate = {}

    def gw_step(n):
        if n == 0:
            total = gwp_ref[pl.ds(cx * 64, 64), :]
            for i in range(3):
                sends.wait(t_gx[i], gx.at[i])
                total = total + gx[i]
            gacc[0] = total
            gstate["z"] = [
                sends.to("z" + name, gacc.at[0, pl.ds(me.up("z", step) * 16, 16)], gz.at[i])
                for i, (step, name) in enumerate(hops)
            ]
        elif n == 1:
            total = gacc[0, pl.ds(cz * 16, 16), :]
            for i in range(3):
                sends.wait(gstate["z"][i], gz.at[i])
                total = total + gz[i]
            gb[0] = total
            gstate["b"] = sends.to("core", gb.at[0], gb.at[3])
        elif n in (2, 3):
            sends.wait(gstate["b"], gb.at[n + 1])
            gb[n - 1] = gb[n - 2] + gb[n + 1]
            gstate["b"] = sends.to(("yh", "y")[n - 2], gb.at[n - 1], gb.at[n + 2])
        elif n == 4:
            sends.wait(gstate["b"], gb.at[5])
            gacc[1, pl.ds(cz * 16, 16), :] = (gb[2] + gb[5]) * f32(1.0 / math.sqrt(65536))
            mine = gacc.at[1, pl.ds(cz * 16, 16)]
            gstate["az"] = [sends.to("z" + name, mine, mine) for _, name in hops]
        elif n == 5:
            for i, (step, _) in enumerate(hops):
                sends.wait(gstate["az"][i], gacc.at[1, pl.ds(me.up("z", -step) * 16, 16)])
            gw_ref[pl.ds(cx * 64, 64), :] = gacc[1]
            mine = piece(cx, 64, gw_ref)
            gstate["ax"] = [sends.to("x" + name, mine, mine) for _, name in hops]
        else:
            for i, (step, _) in enumerate(hops):
                sends.wait(gstate["ax"][i], piece(me.up("x", -step), 64, gw_ref))

    for copy in loads:
        copy.wait()

    slot = {}
    for s in (1, 0):
        for k, d in enumerate(D):
            for p in PARTS:
                slot[s, d, p[2]] = (s * 4 + k) * 2 + p[2]

    E = (2, 1, 3, 0)
    halves, fulls, halves1, fulls1 = {}, {}, {}, {}

    def compute(s, d, p):
        q = slot[s, d, p[2]]

        @pl.loop(0, 4)
        def _(e):
            blk = me.at(ys[s], p[0], d, e)
            rhs = []
            for h in range(16):
                base = blk * 64 + h * 4 + p[2] * 2
                rhs.append(jnp.concatenate([tiles[inv[base]], tiles[inv[base + 1]]], axis=1))
            rhs = jnp.concatenate(rhs, axis=0)
            lhs = jnp.concatenate([bt_ref[i] for i in range(4)], axis=1)
            pbuf[q, e] = jnp.dot(lhs, rhs, preferred_element_type=f32).astype(bf16)

        halves[q] = (
            sends.to(p[1] + "+", pbuf.at[q, 2, lo], in_h.at[q, 0]),
            sends.to(p[1] + "-", pbuf.at[q, 2, hi], in_h.at[q, 1]),
        )

    def second(s, d, p):
        q = slot[s, d, p[2]]
        t = halves[q]
        sends.wait(t[0], in_h.at[q, 0])
        pbuf[q, 1, lo, :] = (pbuf[q, 1, lo, :].astype(f32) + in_h[q, 0].astype(f32)).astype(bf16)
        up = sends.to(p[1] + "+", pbuf.at[q, 1], in_f.at[q, 0])
        sends.wait(t[1], in_h.at[q, 1])
        pbuf[q, 3, hi, :] = (pbuf[q, 3, hi, :].astype(f32) + in_h[q, 1].astype(f32)).astype(bf16)
        down = sends.to(p[1] + "-", pbuf.at[q, 3], in_f.at[q, 1])
        fulls[q] = (up, down)

    def third(s, d, p):
        q = slot[s, d, p[2]]
        t = fulls[q]
        u = s * 2 + p[2]
        sends.wait(t[0], in_f.at[q, 0])
        sends.wait(t[1], in_f.at[q, 1])
        total = pbuf[q, 0].astype(f32) + in_f[q, 0].astype(f32) + in_f[q, 1].astype(f32)
        if d == 2:
            sb[u, 0] = total.astype(bf16)
            halves1[u] = (
                sends.to(p[0] + "+", sb.at[u, 0, lo], in_h1.at[u, 0]),
                sends.to(p[0] + "-", sb.at[u, 0, hi], in_h1.at[u, 1]),
            )
        elif d == 1:
            sb[u, 1] = total.astype(bf16)
            sends.wait(halves1[u][0], in_h1.at[u, 0])
            sb[u, 1, lo, :] = (total[:QUARTER] + in_h1[u, 0].astype(f32)).astype(bf16)
            fulls1[u, 0] = sends.to(p[0] + "+", sb.at[u, 1], in_f1.at[u, 0])
        elif d == -1:
            sb[u, 2] = total.astype(bf16)
            sends.wait(halves1[u][1], in_h1.at[u, 1])
            sb[u, 2, hi, :] = (total[QUARTER:] + in_h1[u, 1].astype(f32)).astype(bf16)
            fulls1[u, 1] = sends.to(p[0] + "-", sb.at[u, 2], in_f1.at[u, 1])
        else:
            tb[p[2]] = total

    to_y = {}

    def fourth(s, p):
        u = s * 2 + p[2]
        for i in range(2):
            sends.wait(fulls1[u, i], in_f1.at[u, i])
        total = tb[p[2]] + in_f1[u, 0].astype(f32) + in_f1[u, 1].astype(f32)
        if s == 1:
            sy[p[2]] = total.astype(bf16)
            to_y[p[2]] = sends.to("y", sy.at[p[2]], in_y.at[p[2]])
        else:
            sends.wait(to_y[p[2]], in_y.at[p[2]])
            total = total + in_y[p[2]].astype(f32)
            gi_ref[pl.ds(p[2] * HALF, HALF), :] = total.T

    steps = [(s, d) for s in (1, 0) for d in D]
    n = len(steps)

    def both(fn, step):
        for p in PARTS:
            fn(*step, p)

    for i in range(n + 2):
        if i < n:
            both(compute, steps[i])
        if 1 <= i <= n:
            both(second, steps[i - 1])
        if i >= 2:
            both(third, steps[i - 2])
            if i - 2 == 3:
                for p in PARTS:
                    fourth(1, p)
        if 1 <= i <= 7:
            gw_step(i - 1)
    for p in PARTS:
        fourth(0, p)
    sends.drain()
    assert sends.count <= 110


def inverse(bands, cols, counts):
    slots = jnp.arange(CAP, dtype=jnp.int32)
    where = jnp.where(slots[None] < counts[:, None], bands * 4 + cols, -1)
    ids = jnp.arange(SLOTS, dtype=jnp.int32).reshape(PANELS, CAP) - SLOTS
    hit = where[:, None, :] == jnp.arange(64, dtype=jnp.int32)[None, :, None]
    return (jnp.sum(jnp.where(hit, ids[:, None, :], 0), axis=2) + SLOTS).reshape(-1)


def local(features, tiles, bands, cols, counts, weight, cotangent):
    inv = inverse(bands[0, 0], cols[0, 0], counts[0, 0])
    tiles = tiles.reshape(SLOTS, BS, BS)
    vmem = pl.BlockSpec(memory_space=pltpu.VMEM)
    hbm = pl.BlockSpec(memory_space=pl.ANY)
    smem = pl.BlockSpec(memory_space=pltpu.SMEM)
    dma = pltpu.SemaphoreType.DMA
    output, gw_part, back = pl.pallas_call(
        forward_kernel,
        out_shape=(
            jax.ShapeDtypeStruct((PANEL, F), bf16),
            jax.ShapeDtypeStruct((F, F), f32),
            jax.ShapeDtypeStruct((4, F, PANEL), bf16),
        ),
        in_specs=[smem, vmem, hbm, vmem, vmem],
        out_specs=(vmem, vmem, vmem),
        scratch_shapes=[
            pltpu.VMEM((PANELS, PANEL, F), bf16),
            pltpu.VMEM((SLOTS + 1, BS, BS), bf16),
            pltpu.VMEM((4, PANEL, F), f32),
            pltpu.VMEM((2, PANEL, F), f32),
            pltpu.VMEM((PANEL, F), bf16),
            pltpu.VMEM((PANEL, F), bf16),
            dma((90,)), dma((90,)), dma((5,)),
        ],
        compiler_params=pltpu.CompilerParams(
            collective_id=0, has_side_effects=True, vmem_limit_bytes=56 * 2**20
        ),
        name="gather_forward",
    )(inv, features, tiles, weight, cotangent)
    grad_input, grad_weight = pl.pallas_call(
        backward_kernel,
        out_shape=(
            jax.ShapeDtypeStruct((PANEL, F), f32),
            jax.ShapeDtypeStruct((F, F), f32),
        ),
        in_specs=[smem, hbm, vmem, vmem],
        out_specs=(vmem, vmem),
        scratch_shapes=[
            pltpu.VMEM((SLOTS + 1, BS, BS), bf16),
            pltpu.VMEM((16, 4, F, HALF), bf16),
            pltpu.VMEM((16, 2, QUARTER, HALF), bf16),
            pltpu.VMEM((16, 2, F, HALF), bf16),
            pltpu.VMEM((4, 3, F, HALF), bf16),
            pltpu.VMEM((4, 2, QUARTER, HALF), bf16),
            pltpu.VMEM((4, 2, F, HALF), bf16),
            pltpu.VMEM((2, F, HALF), f32),
            pltpu.VMEM((2, F, HALF), bf16),
            pltpu.VMEM((2, F, HALF), bf16),
            pltpu.VMEM((3, 64, F), f32),
            pltpu.VMEM((3, 16, F), f32),
            pltpu.VMEM((6, 16, F), f32),
            pltpu.VMEM((2, 64, F), f32),
            dma((110,)), dma((110,)), dma((4,)),
        ],
        compiler_params=pltpu.CompilerParams(
            collective_id=1, has_side_effects=True, vmem_limit_bytes=56 * 2**20
        ),
        name="backward_scatter",
    )(inv, tiles, back, gw_part)
    return output, grad_weight, grad_input


def solution(mesh):
    placed = (
        P(("blk", "rep"), None),
        P("blk", "rep", None, None, None, None),
        P("blk", "rep", None, None),
        P("blk", "rep", None, None),
        P("blk", "rep", None),
        P(),
        P(("blk", "rep"), None),
    )
    return jax.shard_map(
        local,
        mesh=mesh,
        in_specs=placed,
        out_specs=(P(("blk", "rep"), None), P(), P(("blk", "rep"), None)),
        check_vma=False,
    )
```

time: 1390 us -> 169 us (0.12)
  waiting for transfers between devices: 755 us -> 0 us
  matrix products: 267 us -> 0 us
  starting transfers between devices: 212 us -> 0 us
  Pallas kernels: 0 us -> 162 us
  local copies, waits for them, and re-layouts: 87.7 us -> 4.91 us
  other arithmetic: 43 us -> 1.56 us
    ppermute x62 -> x0, waiting for transfers between devices: 559 us -> none  [shifted(): lax.ppermute(shard, axis, [(i, (i + by) % devices) for i in range(devices)])]
    dot_general x131 -> x0, matrix products: 267 us -> none  [the longest x32 104 us: forward_terms(): jnp.einsum('gk,kif->gif', patch_arrangement, product, precision=lax.Preci...]
    ppermute x62 -> x0, starting transfers between devices: 212 us -> none  [shifted(): lax.ppermute(shard, axis, [(i, (i + by) % devices) for i in range(devices)])]
    pallas_call x0 -> x2, Pallas kernels: none -> 162 us  [the longest x1 93.2 us: local(): pl.pallas_call(forward_kernel, out_shape=(jax.ShapeDtypeStruct((PANEL, F)...]
    psum x1 -> x0, waiting for transfers between devices: 143 us -> none  [local(): lax.psum(local_weight, ('blk', 'rep'))]
    convert_element_type x63 -> x0, other arithmetic: 40.1 us -> none  [the longest x31 20.1 us: backward_terms(): (jnp.arange(patch_limit, dtype=jnp.int32) < active_patch_number).astype(j...]
    gather x64 -> x0, local copies, waits for them, and re-layouts: 39.5 us -> none  [the longest x32 20.4 us: backward_terms(): chosen = jnp.take(back_group, block_rows, axis=0)]
    dynamic_slice x64 -> x0, local copies, waits for them, and re-layouts: 39.4 us -> none  [the longest x32 19.8 us: forward_terms(): lax.dynamic_index_in_dim(active_patch_numbers, source, 0, keepdims=False)]
  transfers between devices with their start and end apart: 65 -> 0, of which waited for: 65 -> 0; matrix products, arithmetic and copies ran while one was open for 3% -> 0% of each run, Pallas kernels for 0% -> 0%
where the time goes in v1:
time: 169 us
  Pallas kernels  162 us (96%)
  local copies, waits for them, and re-layouts  4.91 us (3%)
    pallas_call x1, Pallas kernels, local(): pl.pallas_call(forward_kernel, out_shape=(jax.ShapeDtypeStruct((PANEL, F)...  93.2 us
    pallas_call x1, Pallas kernels, local(): pl.pallas_call(backward_kernel, out_shape=(jax.ShapeDtypeStruct((PANEL, F...  68.7 us
    unnamed x5, local copies, waits for them, and re-layouts  4.25 us

profile of v1, /device:TPU:0, one launch (start us, length us, event | category | flops | bytes accessed | tf_op | source)
XLA Modules:
  0.0 169.1 jit_solution(1055713936909136878)
XLA Ops:
  0.6 0.7 multiply_add_fusion
  1.4 0.7 bitcast_select_fusion
  2.0 0.2 select_reduce_fusion
  2.2 0.7 add.34.inv
  2.9 93.2 %gather_forward.1 = (bf16[512,256]{1,0:T(8,128)(2,1)}, f32[256,256]{1,0:T(8,128)}, bf16[4,256,512]{2,1,0:T(8,128)(2,1)}) custom-call(s32[2048]{0:T(1024)} %add.34.inv, bf16[512,256]{1,0:T(8,128)(2,1)} %f_ref.1, bf16[384,128,128]{2,1,0:T(8,128)(2,1)} %bitcast.4, bf16[256,256]{1,0:T(8,128)(2,1)} %w_ref.1, bf16[512,256]{1,0:T(8,128)(2,1)} %ct_ref.1), custom_call_target="tpu_custom_call" | custom-call | tf_op jit(solution)/shard_map/gather_forward/pallas_call | solution.py:454
  96.1 0.0 copy-start
  96.1 68.7 %backward_scatter.1 = (f32[512,256]{1,0:T(8,128)}, f32[256,256]{1,0:T(8,128)}) custom-call(s32[2048]{0:T(1024)} %add.34.inv, bf16[384,128,128]{2,1,0:T(8,128)(2,1)} %bitcast.5, bf16[4,256,512]{2,1,0:T(8,128)(2,1)} %get-tuple-element.9.bt_ref, f32[256,256]{1,0:T(8,128)} %get-tuple-element.10.gwp_ref), custom_call_target="tpu_custom_call" | custom-call | tf_op jit(solution)/shard_map/backward_scatter/pallas_call | solution.py:477
  164.8 0.0 copy-done
  164.8 0.7 copy.16
  165.5 1.7 copy.17
  167.2 1.9 %copy.18 = f32[512,256]{1,0:T(8,128)} copy(f32[512,256]{1,0:T(8,128)} %get-tuple-element.20) | data formatting | bytes 1048576
  (1 shorter events, 0.0 us)
Async XLA Ops:
  96.1 68.7 %copy-start = (bf16[512,256]{1,0:T(8,128)(2,1)S(1)}, bf16[512,256]{1,0:T(8,128)(2,1)}, u32[]{:S(2)}) copy-start(bf16[512,256]{1,0:T(8,128)(2,1)} %get-tuple-element.18) | copy-start | bytes 786436

commit v2 on v1

v2 whole, which is shorter than its diff:
```python
import functools
import math

import jax
import jax.numpy as jnp
from jax import lax
from jax.experimental import pallas as pl
from jax.experimental.pallas import tpu as pltpu
from jax.sharding import PartitionSpec as P

MESH = pl.DeviceIdType.MESH
F = 256
BS = 128
CAP = 12
PANELS = 32
PANEL = 512
HALF = 256
QUARTER = 128
SLOTS = PANELS * CAP
SENDS = 200
bf16 = jnp.bfloat16
f32 = jnp.float32


class Place:
    def __init__(self):
        b = lax.axis_index("blk")
        r = lax.axis_index("rep")
        self.b, self.r = b, r
        self.c = {"x": lax.rem(b, 4), "z": lax.rem(b // 4, 4)}
        self.y = b // 16
        self.yp = 1 - self.y
        self.core = lax.rem(r, 2)
        self.yh = r // 2
        self.nb = {"y": {"blk": self.blk(self.yp, self.c["z"], self.c["x"])}}
        for axis in ("x", "z"):
            for name, step in (("+", 1), ("-", -1), ("2", 2)):
                self.nb[axis + name] = {"blk": self.at(self.y, axis, step, 0)}
        self.nb["core"] = {"rep": self.yh * 2 + 1 - self.core}
        self.nb["yh"] = {"rep": (1 - self.yh) * 2 + self.core}

    def blk(self, y, z, x):
        return y * 16 + z * 4 + x

    def up(self, axis, step):
        return lax.rem(self.c[axis] + step + 4, 4)

    def at(self, y, first, d, e):
        if first == "x":
            return self.blk(y, self.up("z", e), self.up("x", d))
        return self.blk(y, self.up("z", d), self.up("x", e))

    def on_second(self, y, first, d, e):
        if first == "x":
            return self.blk(y, e, self.up("x", d))
        return self.blk(y, self.up("z", d), e)

    def barrier(self, names):
        sem = pltpu.get_barrier_semaphore()
        for name in names:
            pl.semaphore_signal(sem, inc=1, device_id=self.nb[name], device_id_type=MESH)
        pl.semaphore_wait(sem, len(names))


class Sends:
    def __init__(self, place, send, recv):
        self.place, self.send, self.recv = place, send, recv
        self.count = 0
        self.pending = []

    def to(self, where, src, dst):
        t = self.count
        self.count += 1
        copy = pltpu.make_async_remote_copy(
            src, dst, self.send.at[t], self.recv.at[t],
            device_id=self.place.nb[where], device_id_type=MESH,
        )
        copy.start()
        self.pending.append(copy)
        return t

    def wait(self, t, dst):
        pltpu.make_async_remote_copy(
            dst, dst, self.send.at[t], self.recv.at[t],
            device_id=self.place.nb["y"], device_id_type=MESH,
        ).wait_recv()

    def drain(self):
        for copy in self.pending:
            copy.wait_send()


PARTS = (("x", "z", 0), ("z", "x", 1))


def load_tiles(tiles_hbm, tiles, sem):
    copies = [
        pltpu.make_async_copy(
            tiles_hbm.at[pl.ds(i * SLOTS // 4, SLOTS // 4)],
            tiles.at[pl.ds(i * SLOTS // 4, SLOTS // 4)],
            sem.at[i],
        )
        for i in range(4)
    ]
    for copy in copies:
        copy.start()
    return copies


def kernel(
    inv, f_ref, tiles_hbm, w_ref, ct_ref,
    out_ref, gi_ref, gw_ref,
    g, tiles, acc, in1, sbuf, in2, bt, gwp,
    pbuf, in_h, in_f, in_e, sb, in_h1, in_f1, tb, sy, in_y,
    gx, gz, gb, gacc, send, recv, loc,
):
    me = Place()
    me.barrier(("x+", "x-", "x2", "z+", "z-", "z2", "y", "core", "yh"))
    sends = Sends(me, send, recv)
    y, yp = me.y, me.yp
    ys = (y, yp)

    def rows(blk, lo, n):
        return g.at[blk, pl.ds(lo, n)]

    def push(where, blk, lo, n, mine=False):
        src = f_ref.at[pl.ds(lo, n)] if mine else rows(blk, lo, n)
        return sends.to(where, src, rows(blk, lo, n))

    def arrive(t, blk, lo, n):
        sends.wait(t, rows(blk, lo, n))

    p1, p1f, p2, p2f, far2 = {}, {}, {}, {}, {}

    def start2(s, p, d, mine=False):
        blk = me.at(ys[s], p[0], d, 0)
        lo = p[2] * HALF
        p2[s, p[2], d] = (push(p[1] + "+", blk, lo, HALF, mine), push(p[1] + "-", blk, lo, HALF, mine))

    def stage1(s, mine):
        for p in PARTS:
            blk = me.at(ys[s], p[0], 0, 0)
            lo = p[2] * HALF
            p1[s, p[2]] = (push(p[0] + "+", blk, lo, HALF, mine), push(p[0] + "-", blk, lo, HALF, mine))
        for p in PARTS:
            start2(s, p, 0, mine)

    def stage2(s):
        for p in PARTS:
            lo = p[2] * HALF
            t = p1[s, p[2]]
            at = functools.partial(me.at, ys[s], p[0])
            arrive(t[0], at(-1, 0), lo, HALF)
            f0 = push(p[0] + "+", at(-1, 0), lo, QUARTER)
            start2(s, p, -1)
            arrive(t[1], at(1, 0), lo, HALF)
            f1 = push(p[0] + "-", at(1, 0), lo + QUARTER, QUARTER)
            start2(s, p, 1)
            p1f[s, p[2]] = (f0, f1)

    def stage3(s):
        for p in PARTS:
            lo = p[2] * HALF
            f0, f1 = p1f[s, p[2]]
            arrive(f0, me.at(ys[s], p[0], 2, 0), lo, QUARTER)
            arrive(f1, me.at(ys[s], p[0], 2, 0), lo + QUARTER, QUARTER)
            start2(s, p, 2)

    def stage4(s, d):
        for p in PARTS:
            lo = p[2] * HALF
            t = p2[s, p[2], d]
            at = functools.partial(me.at, ys[s], p[0])
            arrive(t[0], at(d, -1), lo, HALF)
            if s == 0:
                f0 = push(p[1] + "+", at(d, -1), lo, QUARTER)
            arrive(t[1], at(d, 1), lo, HALF)
            if s == 0:
                p2f[p[2], d] = (f0, push(p[1] + "-", at(d, 1), lo + QUARTER, QUARTER))

    def stage5(d):
        for p in PARTS:
            lo = p[2] * HALF
            f0, f1 = p2f[p[2], d]
            blk = me.at(y, p[0], d, 2)
            arrive(f0, blk, lo, QUARTER)
            arrive(f1, blk, lo + QUARTER, QUARTER)
            far2[p[2], d] = push("y", blk, lo, HALF)

    def stage6(d):
        for p in PARTS:
            arrive(far2[p[2], d], me.at(yp, p[0], d, 2), p[2] * HALF, HALF)

    def product(hg, s, p, panels):
        lo = p[2] * HALF
        blks = [me.at(ys[s], p[0], d, e) for d, e in panels]
        lhs = []
        for blk in blks:
            for v in range(2):
                base = blk * 64 + hg * 16 + p[2] * 2 + v
                lhs.append(jnp.concatenate([tiles[inv[base + h * 4]] for h in range(4)], axis=0))
        lhs = jnp.concatenate(lhs, axis=1)
        rhs = jnp.concatenate([g[blk, pl.ds(lo, HALF), :] for blk in blks], axis=0)
        return jnp.dot(lhs, rhs, preferred_element_type=f32)

    def compute(s, k, panels, first=False):
        p = PARTS[k]

        @pl.loop(0, 4)
        def _(hg):
            if first:
                acc[hg] = product(hg, s, p, panels)
            else:
                acc[hg] += product(hg, s, p, panels)

    line = ((0, 0), (-1, 0), (1, 0), (2, 0))
    near = ((0, -1), (0, 1), (-1, -1), (-1, 1))
    apart = ((1, -1), (1, 1), (2, -1), (2, 1))
    across = ((0, 2), (-1, 2), (1, 2), (2, 2))

    stage1(0, True)
    to_y = [push("y", me.b, i * HALF, HALF, True) for i in range(2)]
    own = pltpu.make_async_copy(f_ref, g.at[me.b], loc.at[4])
    own.start()
    loads = load_tiles(tiles_hbm, tiles, loc)
    tiles[SLOTS] = jnp.zeros((BS, BS), bf16)
    stage2(0)
    twin = me.blk(yp, me.c["z"], me.c["x"])
    for i in range(2):
        arrive(to_y[i], twin, i * HALF, HALF)
    stage1(1, False)
    stage3(0)
    own.wait()
    for copy in loads:
        copy.wait()
    compute(0, 0, line, True)
    stage2(1)
    compute(0, 1, line)
    stage4(0, 0)
    stage4(0, -1)
    stage3(1)
    compute(0, 0, near)
    stage4(0, 1)
    compute(0, 1, near)
    stage4(0, 2)
    stage5(0)
    compute(1, 0, line)
    stage5(-1)
    compute(1, 1, line)
    stage5(1)
    compute(0, 0, apart)
    stage5(2)
    compute(0, 1, apart)
    compute(0, 0, across)
    compute(0, 1, across)
    stage4(1, 0)
    stage4(1, -1)
    compute(1, 0, near)
    compute(1, 1, near)
    stage4(1, 1)
    stage4(1, 2)
    compute(1, 0, apart)
    compute(1, 1, apart)
    for d in (0, -1, 1, 2):
        stage6(d)

    far = 1 - me.yh
    other = 1 - me.core

    def last(owner):
        @pl.loop(0, 2)
        def _(i):
            hg = owner * 2 + lax.rem(other + i, 2)
            acc[hg] += product(hg, 1, PARTS[0], across)
            acc[hg] += product(hg, 1, PARTS[1], across)

    last(far)
    t_far = sends.to("core", acc.at[far * 2 + other], in1.at[far])
    last(me.yh)
    t_near = sends.to("core", acc.at[me.yh * 2 + other], in1.at[me.yh])
    sends.wait(t_far, in1.at[far])
    t_yh = []
    for i in range(2):
        part = pl.ds(i * HALF, HALF)
        sbuf[i] = (acc[far * 2 + me.core, part, :] + in1[far, part, :]).astype(bf16)
        t_yh.append(sends.to("yh", sbuf.at[i], in2.at[i]))
    sends.wait(t_near, in1.at[me.yh])
    acc[me.r] += in1[me.yh]
    t_bt = []
    for i in range(2):
        part = pl.ds(i * HALF, HALF)
        sends.wait(t_yh[i], in2.at[i])
        agg = (acc[me.r, part, :] + in2[i].astype(f32)).astype(bf16)
        linear = jnp.dot(agg, w_ref[...], preferred_element_type=f32)
        sigma = 1.0 / (1.0 + jnp.exp(-linear))
        gl = (ct_ref[part, :].astype(f32) * sigma * (1.0 + linear * (1.0 - sigma))).astype(bf16)
        back = lax.dot_general(w_ref[...], gl, (((1,), (1,)), ((), ())), preferred_element_type=f32)
        mine = bt.at[me.r * 2 + i]
        bt[me.r * 2 + i] = back.astype(bf16)
        t_bt.append((sends.to("yh", mine, mine), sends.to("core", mine, mine)))
        out_ref[part, :] = (linear * sigma).astype(bf16)
        local_gw = lax.dot_general(agg, gl, (((0,), (0,)), ((), ())), preferred_element_type=f32)
        if i == 0:
            gwp[...] = local_gw
        else:
            gwp[...] += local_gw

    cx, cz = me.c["x"], me.c["z"]

    def piece(axis_x, n, ref):
        return ref.at[pl.ds(axis_x * n, n)]

    hops = ((1, "+"), (2, "2"), (3, "-"))
    gstate = {}

    def gw_step(n):
        if n == 0:
            gstate["x"] = [
                sends.to("x" + name, piece(me.up("x", step), 64, gwp), gx.at[i])
                for i, (step, name) in enumerate(hops)
            ]
        elif n == 1:
            total = gwp[pl.ds(cx * 64, 64), :]
            for i in range(3):
                sends.wait(gstate["x"][i], gx.at[i])
                total = total + gx[i]
            gacc[0] = total
            gstate["z"] = [
                sends.to("z" + name, gacc.at[0, pl.ds(me.up("z", step) * 16, 16)], gz.at[i])
                for i, (step, name) in enumerate(hops)
            ]
        elif n == 2:
            total = gacc[0, pl.ds(cz * 16, 16), :]
            for i in range(3):
                sends.wait(gstate["z"][i], gz.at[i])
                total = total + gz[i]
            gb[0] = total
            gstate["b"] = sends.to("core", gb.at[0], gb.at[3])
        elif n in (3, 4):
            k = n - 3
            sends.wait(gstate["b"], gb.at[k + 3])
            gb[k + 1] = gb[k] + gb[k + 3]
            gstate["b"] = sends.to(("yh", "y")[k], gb.at[k + 1], gb.at[k + 4])
        elif n == 5:
            sends.wait(gstate["b"], gb.at[5])
            gacc[1, pl.ds(cz * 16, 16), :] = (gb[2] + gb[5]) * f32(1.0 / math.sqrt(65536))
            mine = gacc.at[1, pl.ds(cz * 16, 16)]
            gstate["az"] = [sends.to("z" + name, mine, mine) for _, name in hops]
        elif n == 6:
            for i, (step, _) in enumerate(hops):
                sends.wait(gstate["az"][i], gacc.at[1, pl.ds(me.up("z", -step) * 16, 16)])
            gw_ref[pl.ds(cx * 64, 64), :] = gacc[1]
            mine = piece(cx, 64, gw_ref)
            gstate["ax"] = [sends.to("x" + name, mine, mine) for _, name in hops]
        else:
            for i, (step, _) in enumerate(hops):
                sends.wait(gstate["ax"][i], piece(me.up("x", -step), 64, gw_ref))

    there = far * 2 + me.core
    b_fwd = []
    for i in range(2):
        src = bt.at[there * 2 + i]
        sends.wait(t_bt[i][0], src)
        b_fwd.append(sends.to("core", src, src))
    for i in range(2):
        sends.wait(t_bt[i][1], bt.at[(me.yh * 2 + other) * 2 + i])
        sends.wait(b_fwd[i], bt.at[(far * 2 + other) * 2 + i])

    D = (2, -1, 1, 0)
    lo, hi = pl.ds(0, QUARTER), pl.ds(QUARTER, QUARTER)
    halves, fulls, halves1, fulls1, to_e = {}, {}, {}, {}, {}

    def slot(s, d, p):
        return (s * 4 + D.index(d)) * 2 + p[2]

    def wide(ref, *at):
        return ref[at].astype(f32)

    def spread(s, d, p):
        q = slot(s, d, p)

        @pl.loop(0, 4)
        def _(e):
            blk = me.at(ys[s], p[0], d, e)
            rhs = []
            for h in range(16):
                base = blk * 64 + h * 4 + p[2] * 2
                rhs.append(jnp.concatenate([tiles[inv[base]], tiles[inv[base + 1]]], axis=1))
            rhs = jnp.concatenate(rhs, axis=0)
            lhs = jnp.concatenate([bt[i] for i in range(8)], axis=1)
            pbuf[q, e] = jnp.dot(lhs, rhs, preferred_element_type=f32).astype(bf16)

        u = slot(0, d, p)
        if s == 1:
            fulls[q] = (
                sends.to(p[1] + "+", pbuf.at[q, 1], in_f.at[q, 0]),
                sends.to(p[1] + "-", pbuf.at[q, 3], in_f.at[q, 1]),
            )
            to_e[u] = sends.to("y", pbuf.at[q, 2], in_e.at[u])
        else:
            sends.wait(to_e[u], in_e.at[u])
            pbuf[q, 2] = (wide(pbuf, q, 2) + wide(in_e, u)).astype(bf16)
            halves[q] = (
                sends.to(p[1] + "+", pbuf.at[q, 2, lo], in_h.at[q, 0]),
                sends.to(p[1] + "-", pbuf.at[q, 2, hi], in_h.at[q, 1]),
            )

    def second(s, d, p):
        if s == 1:
            return
        q = slot(s, d, p)
        t = halves[q]
        sends.wait(t[0], in_h.at[q, 0])
        pbuf[q, 1, lo, :] = (pbuf[q, 1, lo, :].astype(f32) + wide(in_h, q, 0)).astype(bf16)
        up = sends.to(p[1] + "+", pbuf.at[q, 1], in_f.at[q, 0])
        sends.wait(t[1], in_h.at[q, 1])
        pbuf[q, 3, hi, :] = (pbuf[q, 3, hi, :].astype(f32) + wide(in_h, q, 1)).astype(bf16)
        down = sends.to(p[1] + "-", pbuf.at[q, 3], in_f.at[q, 1])
        fulls[q] = (up, down)

    def third(s, d, p):
        q = slot(s, d, p)
        t = fulls[q]
        u = s * 2 + p[2]
        sends.wait(t[0], in_f.at[q, 0])
        sends.wait(t[1], in_f.at[q, 1])
        total = wide(pbuf, q, 0) + wide(in_f, q, 0) + wide(in_f, q, 1)
        if d == 2:
            sb[u, 0] = total.astype(bf16)
            halves1[u] = (
                sends.to(p[0] + "+", sb.at[u, 0, lo], in_h1.at[u, 0]),
                sends.to(p[0] + "-", sb.at[u, 0, hi], in_h1.at[u, 1]),
            )
        elif d == 1:
            sb[u, 1] = total.astype(bf16)
            sends.wait(halves1[u][0], in_h1.at[u, 0])
            sb[u, 1, lo, :] = (total[:QUARTER] + wide(in_h1, u, 0)).astype(bf16)
            fulls1[u, 0] = sends.to(p[0] + "+", sb.at[u, 1], in_f1.at[u, 0])
        elif d == -1:
            sb[u, 2] = total.astype(bf16)
            sends.wait(halves1[u][1], in_h1.at[u, 1])
            sb[u, 2, hi, :] = (total[QUARTER:] + wide(in_h1, u, 1)).astype(bf16)
            fulls1[u, 1] = sends.to(p[0] + "-", sb.at[u, 2], in_f1.at[u, 1])
        else:
            tb[p[2]] = total

    home = {}

    def fourth(s, p):
        u = s * 2 + p[2]
        for i in range(2):
            sends.wait(fulls1[u, i], in_f1.at[u, i])
        total = tb[p[2]] + wide(in_f1, u, 0) + wide(in_f1, u, 1)
        if s == 1:
            sy[p[2]] = total.astype(bf16)
            home[p[2]] = sends.to("y", sy.at[p[2]], in_y.at[p[2]])
        else:
            sends.wait(home[p[2]], in_y.at[p[2]])
            total = total + wide(in_y, p[2])
            gi_ref[pl.ds(p[2] * HALF, HALF), :] = total.T

    steps = [(s, d) for s in (1, 0) for d in D]
    n = len(steps)

    def both(fn, step):
        for p in PARTS:
            fn(*step, p)

    for i in range(n + 2):
        if i < n:
            both(spread, steps[i])
        if 1 <= i <= n:
            both(second, steps[i - 1])
        if i >= 2:
            both(third, steps[i - 2])
            if i - 2 == 3:
                for p in PARTS:
                    fourth(1, p)
        if i <= 7:
            gw_step(i)
    for p in PARTS:
        fourth(0, p)
    sends.drain()
    assert sends.count <= SENDS


def copy_kernel(*refs):
    k = len(refs) // 2
    for i in range(k):
        refs[k + i][...] = refs[i][...]


def inverse(bands, cols, counts):
    slots = jnp.arange(CAP, dtype=jnp.int32)
    where = jnp.where(slots[None] < counts[:, None], bands * 4 + cols, -1)
    ids = jnp.arange(SLOTS, dtype=jnp.int32).reshape(PANELS, CAP) - SLOTS
    hit = where[:, None, :] == jnp.arange(64, dtype=jnp.int32)[None, :, None]
    return (jnp.sum(jnp.where(hit, ids[:, None, :], 0), axis=2) + SLOTS).reshape(-1)


def local(features, tiles, bands, cols, counts, weight, cotangent):
    inv = inverse(bands[0, 0], cols[0, 0], counts[0, 0])
    tiles = tiles.reshape(SLOTS, BS, BS)
    vmem = pl.BlockSpec(memory_space=pltpu.VMEM)
    hbm = pl.BlockSpec(memory_space=pl.ANY)
    smem = pl.BlockSpec(memory_space=pltpu.SMEM)
    dma = pltpu.SemaphoreType.DMA
    results = (
        jax.ShapeDtypeStruct((PANEL, F), bf16),
        jax.ShapeDtypeStruct((PANEL, F), f32),
        jax.ShapeDtypeStruct((F, F), f32),
    )
    results = pl.pallas_call(
        kernel,
        out_shape=results,
        in_specs=[smem, vmem, hbm, vmem, vmem],
        out_specs=(vmem, vmem, vmem),
        scratch_shapes=[
            pltpu.VMEM((PANELS, PANEL, F), bf16),
            pltpu.VMEM((SLOTS + 1, BS, BS), bf16),
            pltpu.VMEM((4, PANEL, F), f32),
            pltpu.VMEM((2, PANEL, F), f32),
            pltpu.VMEM((2, HALF, F), bf16),
            pltpu.VMEM((2, HALF, F), bf16),
            pltpu.VMEM((8, F, HALF), bf16),
            pltpu.VMEM((F, F), f32),
            pltpu.VMEM((16, 4, F, HALF), bf16),
            pltpu.VMEM((8, 2, QUARTER, HALF), bf16),
            pltpu.VMEM((16, 2, F, HALF), bf16),
            pltpu.VMEM((8, F, HALF), bf16),
            pltpu.VMEM((4, 3, F, HALF), bf16),
            pltpu.VMEM((4, 2, QUARTER, HALF), bf16),
            pltpu.VMEM((4, 2, F, HALF), bf16),
            pltpu.VMEM((2, F, HALF), f32),
            pltpu.VMEM((2, F, HALF), bf16),
            pltpu.VMEM((2, F, HALF), bf16),
            pltpu.VMEM((3, 64, F), f32),
            pltpu.VMEM((3, 16, F), f32),
            pltpu.VMEM((6, 16, F), f32),
            pltpu.VMEM((2, 64, F), f32),
            dma((SENDS,)), dma((SENDS,)), dma((5,)),
        ],
        compiler_params=pltpu.CompilerParams(
            collective_id=0, has_side_effects=True, vmem_limit_bytes=58 * 2**20
        ),
        name="graph_layer",
    )(inv, features, tiles, weight, cotangent)
    output, grad_input, grad_weight = pl.pallas_call(
        copy_kernel,
        out_shape=tuple(jax.ShapeDtypeStruct(x.shape, x.dtype) for x in results),
        in_specs=[vmem] * 3,
        out_specs=(vmem,) * 3,
        name="results",
    )(*results)
    return output, grad_weight, grad_input


def solution(mesh):
    placed = (
        P(("blk", "rep"), None),
        P("blk", "rep", None, None, None, None),
        P("blk", "rep", None, None),
        P("blk", "rep", None, None),
        P("blk", "rep", None),
        P(),
        P(("blk", "rep"), None),
    )
    return jax.shard_map(
        local,
        mesh=mesh,
        in_specs=placed,
        out_specs=(P(("blk", "rep"), None), P(), P(("blk", "rep"), None)),
        check_vma=False,
    )
```

time: 169 us -> 150 us (0.89)
  Pallas kernels: 162 us -> 147 us
  local copies, waits for them, and re-layouts: 4.91 us -> 0.67 us
    pallas_call x2, Pallas kernels: 162 us -> 147 us  [the longest x1 145 us: local(): pl.pallas_call(kernel, out_shape=results, in_specs=[smem, vmem, hbm, vmem...]
    unnamed x5 -> x0, local copies, waits for them, and re-layouts: 4.25 us -> none
where the time goes in v2:
time: 150 us
  Pallas kernels  147 us (98%)
  other arithmetic  1.56 us (1%)
    pallas_call x1, Pallas kernels, local(): pl.pallas_call(kernel, out_shape=results, in_specs=[smem, vmem, hbm, vmem...  145 us

profile of v2, /device:TPU:0, one launch (start us, length us, event | category | flops | bytes accessed | tf_op | source)
XLA Modules:
  0.0 150.0 jit_solution(3370443692975942849)
XLA Ops:
  0.6 0.7 multiply_add_fusion
  1.4 0.7 bitcast_select_fusion
  2.0 0.2 select_reduce_fusion
  2.2 0.7 add.34.inv
  2.9 145.0 %graph_layer.1 = (bf16[512,256]{1,0:T(8,128)(2,1)}, f32[512,256]{1,0:T(8,128)}, f32[256,256]{1,0:T(8,128)}) custom-call(s32[2048]{0:T(1024)} %add.34.inv, bf16[512,256]{1,0:T(8,128)(2,1)} %f_ref.1, bf16[384,128,128]{2,1,0:T(8,128)(2,1)} %bitcast.4, bf16[256,256]{1,0:T(8,128)(2,1)} %w_ref.1, bf16[512,256]{1,0:T(8,128)(2,1)} %ct_ref.1), custom_call_target="tpu_custom_call" | custom-call | tf_op jit(solution)/shard_map/graph_layer/pallas_call | solution.py:513
  147.9 2.2 %results.1 = (bf16[512,256]{1,0:T(8,128)(2,1)}, f32[512,256]{1,0:T(8,128)}, f32[256,256]{1,0:T(8,128)}) custom-call(bf16[512,256]{1,0:T(8,128)(2,1)} %get-tuple-element.9.refs_0_, f32[512,256]{1,0:T(8,128)} %get-tuple-element.10.refs_1_, f32[256,256]{1,0:T(8,128)} %get-tuple-element.11.refs_2_), custom_call_target="tpu_custom_call" | custom-call | tf_op jit(solution)/shard_map/results/pallas_call | solution.py:548
  (1 shorter events, 0.0 us)

commit v3 on v2

--- a/solution.py
+++ b/solution.py
@@ -130,12 +130,13 @@
     def arrive(t, blk, lo, n):
         sends.wait(t, rows(blk, lo, n))
 
-    p1, p1f, p2, p2f, far2 = {}, {}, {}, {}, {}
+    p1, p1f, p2, p2f, far2, far3 = {}, {}, {}, {}, {}, {}
 
     def start2(s, p, d, mine=False):
         blk = me.at(ys[s], p[0], d, 0)
         lo = p[2] * HALF
-        p2[s, p[2], d] = (push(p[1] + "+", blk, lo, HALF, mine), push(p[1] + "-", blk, lo, HALF, mine))
+        down = push(p[1] + "-", blk, lo, HALF, mine)
+        p2[s, p[2], d] = (push(p[1] + "+", blk, lo, HALF, mine) if s == 0 else None, down)
 
     def stage1(s, mine):
         for p in PARTS:
@@ -166,57 +167,56 @@
             arrive(f1, me.at(ys[s], p[0], 2, 0), lo + QUARTER, QUARTER)
             start2(s, p, 2)
 
-    def stage4(s, d):
+    def stage4(d):
         for p in PARTS:
             lo = p[2] * HALF
-            t = p2[s, p[2], d]
-            at = functools.partial(me.at, ys[s], p[0])
+            t = p2[0, p[2], d]
+            at = functools.partial(me.at, y, p[0])
             arrive(t[0], at(d, -1), lo, HALF)
-            if s == 0:
-                f0 = push(p[1] + "+", at(d, -1), lo, QUARTER)
+            far2[p[2], d] = push("y", at(d, -1), lo, HALF)
+            f0 = push(p[1] + "+", at(d, -1), lo, QUARTER)
             arrive(t[1], at(d, 1), lo, HALF)
-            if s == 0:
-                p2f[p[2], d] = (f0, push(p[1] + "-", at(d, 1), lo + QUARTER, QUARTER))
+            p2f[p[2], d] = (f0, push(p[1] + "-", at(d, 1), lo + QUARTER, QUARTER))
 
     def stage5(d):
         for p in PARTS:
             lo = p[2] * HALF
-            f0, f1 = p2f[p[2], d]
             blk = me.at(y, p[0], d, 2)
-            arrive(f0, blk, lo, QUARTER)
-            arrive(f1, blk, lo + QUARTER, QUARTER)
-            far2[p[2], d] = push("y", blk, lo, HALF)
+            arrive(p2f[p[2], d][0], blk, lo, QUARTER)
+            arrive(p2f[p[2], d][1], blk, lo + QUARTER, QUARTER)
 
     def stage6(d):
         for p in PARTS:
-            arrive(far2[p[2], d], me.at(yp, p[0], d, 2), p[2] * HALF, HALF)
-
-    def product(hg, s, p, panels):
-        lo = p[2] * HALF
-        blks = [me.at(ys[s], p[0], d, e) for d, e in panels]
+            blk = me.at(yp, p[0], d, -1)
+            arrive(far2[p[2], d], blk, p[2] * HALF, HALF)
+            far3[p[2], d] = push(p[1] + "+", blk, p[2] * HALF, HALF)
+
+    def stage7(d):
+        for p in PARTS:
+            arrive(p2[1, p[2], d][1], me.at(yp, p[0], d, 1), p[2] * HALF, HALF)
+
+    def stage8(d):
+        for p in PARTS:
+            arrive(far3[p[2], d], me.at(yp, p[0], d, 2), p[2] * HALF, HALF)
+
+    def product(half, s, panels):
+        blks = [(me.at(ys[s], p[0], d, e), p[2]) for d, e in panels for p in PARTS]
         lhs = []
-        for blk in blks:
+        for blk, k in blks:
             for v in range(2):
-                base = blk * 64 + hg * 16 + p[2] * 2 + v
-                lhs.append(jnp.concatenate([tiles[inv[base + h * 4]] for h in range(4)], axis=0))
+                base = blk * 64 + half * 32 + k * 2 + v
+                lhs.append(jnp.concatenate([tiles[inv[base + h * 4]] for h in range(8)], axis=0))
         lhs = jnp.concatenate(lhs, axis=1)
-        rhs = jnp.concatenate([g[blk, pl.ds(lo, HALF), :] for blk in blks], axis=0)
+        rhs = jnp.concatenate([g[blk, pl.ds(k * HALF, HALF), :] for blk, k in blks], axis=0)
         return jnp.dot(lhs, rhs, preferred_element_type=f32)
 
-    def compute(s, k, panels, first=False):
-        p = PARTS[k]
-
-        @pl.loop(0, 4)
-        def _(hg):
+    def compute(s, *panels, first=False):
+        @pl.loop(0, 2)
+        def _(half):
             if first:
-                acc[hg] = product(hg, s, p, panels)
+                acc[half] = product(half, s, panels)
             else:
-                acc[hg] += product(hg, s, p, panels)
-
-    line = ((0, 0), (-1, 0), (1, 0), (2, 0))
-    near = ((0, -1), (0, 1), (-1, -1), (-1, 1))
-    apart = ((1, -1), (1, 1), (2, -1), (2, 1))
-    across = ((0, 2), (-1, 2), (1, 2), (2, 2))
+                acc[half] += product(half, s, panels)
 
     stage1(0, True)
     to_y = [push("y", me.b, i * HALF, HALF, True) for i in range(2)]
@@ -225,72 +225,77 @@
     loads = load_tiles(tiles_hbm, tiles, loc)
     tiles[SLOTS] = jnp.zeros((BS, BS), bf16)
     stage2(0)
+    own.wait()
+    for copy in loads:
+        copy.wait()
+    compute(0, (0, 0), (-1, 0), first=True)
+    stage4(0)
     twin = me.blk(yp, me.c["z"], me.c["x"])
     for i in range(2):
         arrive(to_y[i], twin, i * HALF, HALF)
     stage1(1, False)
     stage3(0)
-    own.wait()
-    for copy in loads:
-        copy.wait()
-    compute(0, 0, line, True)
+    compute(0, (0, -1), (0, 1))
+    compute(0, (1, 0), (2, 0))
+    stage4(-1)
+    compute(0, (-1, -1), (-1, 1))
+    stage4(1)
+    stage6(0)
+    compute(0, (1, -1), (1, 1))
     stage2(1)
-    compute(0, 1, line)
-    stage4(0, 0)
-    stage4(0, -1)
+    stage5(0)
+    compute(1, (0, 0), (-1, 0))
+    stage6(-1)
+    stage4(2)
     stage3(1)
-    compute(0, 0, near)
-    stage4(0, 1)
-    compute(0, 1, near)
-    stage4(0, 2)
-    stage5(0)
-    compute(1, 0, line)
     stage5(-1)
-    compute(1, 1, line)
+    compute(0, (2, -1), (2, 1))
+    stage6(1)
+    compute(0, (0, 2), (-1, 2))
+    compute(1, (1, 0), (2, 0))
     stage5(1)
-    compute(0, 0, apart)
+    stage6(2)
     stage5(2)
-    compute(0, 1, apart)
-    compute(0, 0, across)
-    compute(0, 1, across)
-    stage4(1, 0)
-    stage4(1, -1)
-    compute(1, 0, near)
-    compute(1, 1, near)
-    stage4(1, 1)
-    stage4(1, 2)
-    compute(1, 0, apart)
-    compute(1, 1, apart)
-    for d in (0, -1, 1, 2):
-        stage6(d)
+    compute(0, (1, 2), (2, 2))
+    compute(1, (0, -1), (-1, -1))
+    compute(1, (1, -1), (2, -1))
+    for d in (0, -1):
+        stage7(d)
+    compute(1, (0, 1), (-1, 1))
+    for d in (1, 2):
+        stage7(d)
+    compute(1, (1, 1), (2, 1))
+    for d in (0, -1):
+        stage8(d)
+    compute(1, (0, 2), (-1, 2))
+    for d in (1, 2):
+        stage8(d)
 
     far = 1 - me.yh
     other = 1 - me.core
 
-    def last(owner):
-        @pl.loop(0, 2)
-        def _(i):
-            hg = owner * 2 + lax.rem(other + i, 2)
-            acc[hg] += product(hg, 1, PARTS[0], across)
-            acc[hg] += product(hg, 1, PARTS[1], across)
-
+    def last(half):
+        acc[half] += product(half, 1, ((1, 2), (2, 2)))
+
+    theirs = pl.ds(other * PANEL, PANEL)
     last(far)
-    t_far = sends.to("core", acc.at[far * 2 + other], in1.at[far])
+    t_far = sends.to("core", acc.at[far, theirs], in1.at[far])
     last(me.yh)
-    t_near = sends.to("core", acc.at[me.yh * 2 + other], in1.at[me.yh])
+    t_near = sends.to("core", acc.at[me.yh, theirs], in1.at[me.yh])
     sends.wait(t_far, in1.at[far])
     t_yh = []
     for i in range(2):
         part = pl.ds(i * HALF, HALF)
-        sbuf[i] = (acc[far * 2 + me.core, part, :] + in1[far, part, :]).astype(bf16)
+        mine = acc[far, pl.ds(me.core * PANEL + i * HALF, HALF), :]
+        sbuf[i] = (mine + in1[far, part, :]).astype(bf16)
         t_yh.append(sends.to("yh", sbuf.at[i], in2.at[i]))
     sends.wait(t_near, in1.at[me.yh])
-    acc[me.r] += in1[me.yh]
     t_bt = []
     for i in range(2):
         part = pl.ds(i * HALF, HALF)
         sends.wait(t_yh[i], in2.at[i])
-        agg = (acc[me.r, part, :] + in2[i].astype(f32)).astype(bf16)
+        mine = acc[me.yh, pl.ds(me.core * PANEL + i * HALF, HALF), :]
+        agg = (mine + in1[me.yh, part, :] + in2[i].astype(f32)).astype(bf16)
         linear = jnp.dot(agg, w_ref[...], preferred_element_type=f32)
         sigma = 1.0 / (1.0 + jnp.exp(-linear))
         gl = (ct_ref[part, :].astype(f32) * sigma * (1.0 + linear * (1.0 - sigma))).astype(bf16)
@@ -379,31 +384,36 @@
     def spread(s, d, p):
         q = slot(s, d, p)
 
-        @pl.loop(0, 4)
-        def _(e):
-            blk = me.at(ys[s], p[0], d, e)
-            rhs = []
-            for h in range(16):
-                base = blk * 64 + h * 4 + p[2] * 2
-                rhs.append(jnp.concatenate([tiles[inv[base]], tiles[inv[base + 1]]], axis=1))
-            rhs = jnp.concatenate(rhs, axis=0)
+        def pair(*es):
+            cols = []
+            for e in es:
+                base = me.at(ys[s], p[0], d, e) * 64 + p[2] * 2
+                for v in range(2):
+                    cols.append(jnp.concatenate([tiles[inv[base + v + h * 4]] for h in range(16)], axis=0))
+            rhs = jnp.concatenate(cols, axis=1)
             lhs = jnp.concatenate([bt[i] for i in range(8)], axis=1)
-            pbuf[q, e] = jnp.dot(lhs, rhs, preferred_element_type=f32).astype(bf16)
+            both = jnp.dot(lhs, rhs, preferred_element_type=f32).astype(bf16)
+            for i, e in enumerate(es):
+                pbuf[q, e] = both[:, i * HALF:(i + 1) * HALF]
 
         u = slot(0, d, p)
         if s == 1:
+            pair(1, 3)
             fulls[q] = (
                 sends.to(p[1] + "+", pbuf.at[q, 1], in_f.at[q, 0]),
                 sends.to(p[1] + "-", pbuf.at[q, 3], in_f.at[q, 1]),
             )
+            pair(2, 0)
             to_e[u] = sends.to("y", pbuf.at[q, 2], in_e.at[u])
         else:
+            pair(2, 1)
             sends.wait(to_e[u], in_e.at[u])
             pbuf[q, 2] = (wide(pbuf, q, 2) + wide(in_e, u)).astype(bf16)
             halves[q] = (
                 sends.to(p[1] + "+", pbuf.at[q, 2, lo], in_h.at[q, 0]),
                 sends.to(p[1] + "-", pbuf.at[q, 2, hi], in_h.at[q, 1]),
             )
+            pair(3, 0)
 
     def second(s, d, p):
         if s == 1:
@@ -518,7 +528,7 @@
         scratch_shapes=[
             pltpu.VMEM((PANELS, PANEL, F), bf16),
             pltpu.VMEM((SLOTS + 1, BS, BS), bf16),
-            pltpu.VMEM((4, PANEL, F), f32),
+            pltpu.VMEM((2, 2 * PANEL, F), f32),
             pltpu.VMEM((2, PANEL, F), f32),
             pltpu.VMEM((2, HALF, F), bf16),
             pltpu.VMEM((2, HALF, F), bf16),

time: 150 us -> 139 us (0.927)
  Pallas kernels: 147 us -> 135 us
    pallas_call x1, Pallas kernels: 145 us -> 133 us  [local(): pl.pallas_call(kernel, out_shape=results, in_specs=[smem, vmem, hbm, vmem...]
where the time goes in v3:
time: 139 us; the launch traced here: 138 us
  Pallas kernels  135 us (97%)
  other arithmetic  1.56 us (1%)
    pallas_call x1, Pallas kernels, local(): pl.pallas_call(kernel, out_shape=results, in_specs=[smem, vmem, hbm, vmem...  133 us

profile of v3, /device:TPU:0, one launch (start us, length us, event | category | flops | bytes accessed | tf_op | source)
XLA Modules:
  0.0 138.2 jit_solution(8357510336625197415)
XLA Ops:
  0.6 0.7 multiply_add_fusion
  1.4 0.7 bitcast_select_fusion
  2.0 0.2 select_reduce_fusion
  2.2 0.7 add.34.inv
  2.9 133.2 %graph_layer.1 = (bf16[512,256]{1,0:T(8,128)(2,1)}, f32[512,256]{1,0:T(8,128)}, f32[256,256]{1,0:T(8,128)}) custom-call(s32[2048]{0:T(1024)} %add.34.inv, bf16[512,256]{1,0:T(8,128)(2,1)} %f_ref.1, bf16[384,128,128]{2,1,0:T(8,128)(2,1)} %bitcast.4, bf16[256,256]{1,0:T(8,128)(2,1)} %w_ref.1, bf16[512,256]{1,0:T(8,128)(2,1)} %ct_ref.1), custom_call_target="tpu_custom_call" | custom-call | tf_op jit(solution)/shard_map/graph_layer/pallas_call | solution.py:523
  136.0 2.2 %results.1 = (bf16[512,256]{1,0:T(8,128)(2,1)}, f32[512,256]{1,0:T(8,128)}, f32[256,256]{1,0:T(8,128)}) custom-call(bf16[512,256]{1,0:T(8,128)(2,1)} %get-tuple-element.9.refs_0_, f32[512,256]{1,0:T(8,128)} %get-tuple-element.10.refs_1_, f32[256,256]{1,0:T(8,128)} %get-tuple-element.11.refs_2_), custom_call_target="tpu_custom_call" | custom-call | tf_op jit(solution)/shard_map/results/pallas_call | solution.py:558
  (1 shorter events, 0.0 us)

commit v4 on v3

--- a/solution.py
+++ b/solution.py
@@ -112,7 +112,7 @@
     out_ref, gi_ref, gw_ref,
     g, tiles, acc, in1, sbuf, in2, bt, gwp,
     pbuf, in_h, in_f, in_e, sb, in_h1, in_f1, tb, sy, in_y,
-    gx, gz, gb, gacc, send, recv, loc,
+    gc, ga, gy, gq, gx, gz, gb, gr, go, send, recv, loc,
 ):
     me = Place()
     me.barrier(("x+", "x-", "x2", "z+", "z-", "z2", "y", "core", "yh"))
@@ -204,8 +204,8 @@
         lhs = []
         for blk, k in blks:
             for v in range(2):
-                base = blk * 64 + half * 32 + k * 2 + v
-                lhs.append(jnp.concatenate([tiles[inv[base + h * 4]] for h in range(8)], axis=0))
+                base = half * 32 + k * 2 + v
+                lhs.append(jnp.concatenate([tiles[inv[blk, base + h * 4]] for h in range(8)], axis=0))
         lhs = jnp.concatenate(lhs, axis=1)
         rhs = jnp.concatenate([g[blk, pl.ds(k * HALF, HALF), :] for blk, k in blks], axis=0)
         return jnp.dot(lhs, rhs, preferred_element_type=f32)
@@ -217,6 +217,19 @@
                 acc[half] = product(half, s, panels)
             else:
                 acc[half] += product(half, s, panels)
+
+    far = 1 - me.yh
+    other = 1 - me.core
+    later = []
+
+    def first_far(s, *panels):
+        acc[far] += product(far, s, panels)
+        later.append((s, panels))
+
+    def catch_up(n):
+        for s, panels in later[:n]:
+            acc[me.yh] += product(me.yh, s, panels)
+        del later[:n]
 
     stage1(0, True)
     to_y = [push("y", me.b, i * HALF, HALF, True) for i in range(2)]
@@ -256,32 +269,25 @@
     stage5(1)
     stage6(2)
     stage5(2)
-    compute(0, (1, 2), (2, 2))
-    compute(1, (0, -1), (-1, -1))
-    compute(1, (1, -1), (2, -1))
+    first_far(0, (1, 2), (2, 2))
+    first_far(1, (0, -1), (-1, -1))
+    first_far(1, (1, -1), (2, -1))
     for d in (0, -1):
         stage7(d)
-    compute(1, (0, 1), (-1, 1))
+    first_far(1, (0, 1), (-1, 1))
     for d in (1, 2):
         stage7(d)
-    compute(1, (1, 1), (2, 1))
+    first_far(1, (1, 1), (2, 1))
     for d in (0, -1):
         stage8(d)
-    compute(1, (0, 2), (-1, 2))
+    first_far(1, (0, 2), (-1, 2))
     for d in (1, 2):
         stage8(d)
-
-    far = 1 - me.yh
-    other = 1 - me.core
-
-    def last(half):
-        acc[half] += product(half, 1, ((1, 2), (2, 2)))
+    first_far(1, (1, 2), (2, 2))
 
     theirs = pl.ds(other * PANEL, PANEL)
-    last(far)
     t_far = sends.to("core", acc.at[far, theirs], in1.at[far])
-    last(me.yh)
-    t_near = sends.to("core", acc.at[me.yh, theirs], in1.at[me.yh])
+    catch_up(3)
     sends.wait(t_far, in1.at[far])
     t_yh = []
     for i in range(2):
@@ -289,6 +295,8 @@
         mine = acc[far, pl.ds(me.core * PANEL + i * HALF, HALF), :]
         sbuf[i] = (mine + in1[far, part, :]).astype(bf16)
         t_yh.append(sends.to("yh", sbuf.at[i], in2.at[i]))
+    catch_up(len(later))
+    t_near = sends.to("core", acc.at[me.yh, theirs], in1.at[me.yh])
     sends.wait(t_near, in1.at[me.yh])
     t_bt = []
     for i in range(2):
@@ -311,55 +319,54 @@
             gwp[...] += local_gw
 
     cx, cz = me.c["x"], me.c["z"]
-
-    def piece(axis_x, n, ref):
-        return ref.at[pl.ds(axis_x * n, n)]
-
     hops = ((1, "+"), (2, "2"), (3, "-"))
     gstate = {}
 
     def gw_step(n):
+        t = gstate.get("t")
         if n == 0:
-            gstate["x"] = [
-                sends.to("x" + name, piece(me.up("x", step), 64, gwp), gx.at[i])
+            gstate["t"] = sends.to("core", gwp.at[pl.ds(other * 128, 128)], gc)
+        elif n == 1:
+            sends.wait(t, gc)
+            ga[...] = gwp[pl.ds(me.core * 128, 128), :] + gc[...]
+            gstate["t"] = sends.to("y", ga.at[pl.ds(yp * 64, 64)], gy)
+        elif n == 2:
+            sends.wait(t, gy)
+            gq[...] = ga[pl.ds(y * 64, 64), :] + gy[...]
+            gstate["t"] = [
+                sends.to("x" + name, gq.at[pl.ds(me.up("x", step) * 16, 16)], gx.at[i])
                 for i, (step, name) in enumerate(hops)
             ]
-        elif n == 1:
-            total = gwp[pl.ds(cx * 64, 64), :]
+        elif n == 3:
+            total = gq[pl.ds(cx * 16, 16), :]
             for i in range(3):
-                sends.wait(gstate["x"][i], gx.at[i])
+                sends.wait(t[i], gx.at[i])
                 total = total + gx[i]
-            gacc[0] = total
-            gstate["z"] = [
-                sends.to("z" + name, gacc.at[0, pl.ds(me.up("z", step) * 16, 16)], gz.at[i])
-                for i, (step, name) in enumerate(hops)
-            ]
-        elif n == 2:
-            total = gacc[0, pl.ds(cz * 16, 16), :]
-            for i in range(3):
-                sends.wait(gstate["z"][i], gz.at[i])
-                total = total + gz[i]
-            gb[0] = total
-            gstate["b"] = sends.to("core", gb.at[0], gb.at[3])
-        elif n in (3, 4):
-            k = n - 3
-            sends.wait(gstate["b"], gb.at[k + 3])
-            gb[k + 1] = gb[k] + gb[k + 3]
-            gstate["b"] = sends.to(("yh", "y")[k], gb.at[k + 1], gb.at[k + 4])
+            gz[cz] = total
+            gstate["t"] = [sends.to("z" + name, gz.at[cz], gz.at[cz]) for _, name in hops]
+        elif n == 4:
+            for i, (step, _) in enumerate(hops):
+                sends.wait(t[i], gz.at[me.up("z", -step)])
+            gb[0] = (gz[0] + gz[1]) + (gz[2] + gz[3])
+            gstate["t"] = sends.to("yh", gb.at[0], gb.at[1])
         elif n == 5:
-            sends.wait(gstate["b"], gb.at[5])
-            gacc[1, pl.ds(cz * 16, 16), :] = (gb[2] + gb[5]) * f32(1.0 / math.sqrt(65536))
-            mine = gacc.at[1, pl.ds(cz * 16, 16)]
-            gstate["az"] = [sends.to("z" + name, mine, mine) for _, name in hops]
+            sends.wait(t, gb.at[1])
+            gr[pl.ds(cx * 16, 16), :] = (gb[0] + gb[1]) * f32(1.0 / math.sqrt(65536))
+            mine = gr.at[pl.ds(cx * 16, 16)]
+            gstate["t"] = [sends.to("x" + name, mine, mine) for _, name in hops]
         elif n == 6:
             for i, (step, _) in enumerate(hops):
-                sends.wait(gstate["az"][i], gacc.at[1, pl.ds(me.up("z", -step) * 16, 16)])
-            gw_ref[pl.ds(cx * 64, 64), :] = gacc[1]
-            mine = piece(cx, 64, gw_ref)
-            gstate["ax"] = [sends.to("x" + name, mine, mine) for _, name in hops]
-        else:
-            for i, (step, _) in enumerate(hops):
-                sends.wait(gstate["ax"][i], piece(me.up("x", -step), 64, gw_ref))
+                sends.wait(t[i], gr.at[pl.ds(me.up("x", -step) * 16, 16)])
+            go[pl.ds(y * 64, 64), :] = gr[...]
+            mine = go.at[pl.ds(y * 64, 64)]
+            gstate["t"] = sends.to("y", mine, mine)
+        elif n == 7:
+            sends.wait(t, go.at[pl.ds(yp * 64, 64)])
+            gw_ref[pl.ds(me.core * 128, 128), :] = go[...]
+            mine = gw_ref.at[pl.ds(me.core * 128, 128)]
+            gstate["t"] = sends.to("core", mine, mine)
+        elif n == 8:
+            sends.wait(t, gw_ref.at[pl.ds(other * 128, 128)])
 
     there = far * 2 + me.core
     b_fwd = []
@@ -387,9 +394,9 @@
         def pair(*es):
             cols = []
             for e in es:
-                base = me.at(ys[s], p[0], d, e) * 64 + p[2] * 2
+                blk = me.at(ys[s], p[0], d, e)
                 for v in range(2):
-                    cols.append(jnp.concatenate([tiles[inv[base + v + h * 4]] for h in range(16)], axis=0))
+                    cols.append(jnp.concatenate([tiles[inv[blk, p[2] * 2 + v + h * 4]] for h in range(16)], axis=0))
             rhs = jnp.concatenate(cols, axis=1)
             lhs = jnp.concatenate([bt[i] for i in range(8)], axis=1)
             both = jnp.dot(lhs, rhs, preferred_element_type=f32).astype(bf16)
@@ -486,8 +493,7 @@
             if i - 2 == 3:
                 for p in PARTS:
                     fourth(1, p)
-        if i <= 7:
-            gw_step(i)
+        gw_step(i)
     for p in PARTS:
         fourth(0, p)
     sends.drain()
@@ -505,7 +511,7 @@
     where = jnp.where(slots[None] < counts[:, None], bands * 4 + cols, -1)
     ids = jnp.arange(SLOTS, dtype=jnp.int32).reshape(PANELS, CAP) - SLOTS
     hit = where[:, None, :] == jnp.arange(64, dtype=jnp.int32)[None, :, None]
-    return (jnp.sum(jnp.where(hit, ids[:, None, :], 0), axis=2) + SLOTS).reshape(-1)
+    return jnp.sum(jnp.where(hit, ids[:, None, :], 0), axis=2) + SLOTS
 
 
 def local(features, tiles, bands, cols, counts, weight, cotangent):
@@ -544,10 +550,15 @@
             pltpu.VMEM((2, F, HALF), f32),
             pltpu.VMEM((2, F, HALF), bf16),
             pltpu.VMEM((2, F, HALF), bf16),
-            pltpu.VMEM((3, 64, F), f32),
+            pltpu.VMEM((128, F), f32),
+            pltpu.VMEM((128, F), f32),
+            pltpu.VMEM((64, F), f32),
+            pltpu.VMEM((64, F), f32),
             pltpu.VMEM((3, 16, F), f32),
-            pltpu.VMEM((6, 16, F), f32),
-            pltpu.VMEM((2, 64, F), f32),
+            pltpu.VMEM((4, 16, F), f32),
+            pltpu.VMEM((2, 16, F), f32),
+            pltpu.VMEM((64, F), f32),
+            pltpu.VMEM((128, F), f32),
             dma((SENDS,)), dma((SENDS,)), dma((5,)),
         ],
         compiler_params=pltpu.CompilerParams(

time: 139 us -> 134 us (0.964)
  Pallas kernels: 135 us -> 131 us
    pallas_call x1, Pallas kernels: 133 us -> 129 us  [local(): pl.pallas_call(kernel, out_shape=results, in_specs=[smem, vmem, hbm, vmem...]
where the time goes in v4:
time: 134 us
  Pallas kernels  131 us (98%)
  other arithmetic  2.16 us (2%)
    pallas_call x1, Pallas kernels, local(): pl.pallas_call(kernel, out_shape=results, in_specs=[smem, vmem, hbm, vmem...  129 us

profile of v4, /device:TPU:0, one launch (start us, length us, event | category | flops | bytes accessed | tf_op | source)
XLA Modules:
  0.0 134.0 jit_solution(10607833207932666264)
XLA Ops:
  0.6 0.7 multiply_add_fusion
  1.4 0.7 bitcast_select_fusion
  2.0 0.2 select_reduce_fusion
  2.2 0.6 broadcast_add_fusion.inv
  2.8 129.1 %graph_layer.1 = (bf16[512,256]{1,0:T(8,128)(2,1)}, f32[512,256]{1,0:T(8,128)}, f32[256,256]{1,0:T(8,128)}) custom-call(s32[32,64]{1,0:T(8,128)} %broadcast_add_fusion.inv, bf16[512,256]{1,0:T(8,128)(2,1)} %f_ref.1, bf16[384,128,128]{2,1,0:T(8,128)(2,1)} %bitcast.4, bf16[256,256]{1,0:T(8,128)(2,1)} %w_ref.1, bf16[512,256]{1,0:T(8,128)(2,1)} %ct_ref.1), custom_call_target="tpu_custom_call" | custom-call | tf_op jit(solution)/shard_map/graph_layer/pallas_call | solution.py:529
  131.9 2.2 %results.1 = (bf16[512,256]{1,0:T(8,128)(2,1)}, f32[512,256]{1,0:T(8,128)}, f32[256,256]{1,0:T(8,128)}) custom-call(bf16[512,256]{1,0:T(8,128)(2,1)} %get-tuple-element.9.refs_0_, f32[512,256]{1,0:T(8,128)} %get-tuple-element.10.refs_1_, f32[256,256]{1,0:T(8,128)} %get-tuple-element.11.refs_2_), custom_call_target="tpu_custom_call" | custom-call | tf_op jit(solution)/shard_map/results/pallas_call | solution.py:569

commit v5 on v4

--- a/solution.py
+++ b/solution.py
@@ -18,6 +18,7 @@
 QUARTER = 128
 SLOTS = PANELS * CAP
 SENDS = 200
+GW_AT = {1: 2, 2: 3, 3: 4, 6: 5, 7: 6, 9: 7}
 bf16 = jnp.bfloat16
 f32 = jnp.float32
 
@@ -368,6 +369,7 @@
         elif n == 8:
             sends.wait(t, gw_ref.at[pl.ds(other * 128, 128)])
 
+    gw_step(0)
     there = far * 2 + me.core
     b_fwd = []
     for i in range(2):
@@ -483,6 +485,7 @@
         for p in PARTS:
             fn(*step, p)
 
+    gw_step(1)
     for i in range(n + 2):
         if i < n:
             both(spread, steps[i])
@@ -493,9 +496,11 @@
             if i - 2 == 3:
                 for p in PARTS:
                     fourth(1, p)
-        gw_step(i)
+        if i in GW_AT:
+            gw_step(GW_AT[i])
     for p in PARTS:
         fourth(0, p)
+    gw_step(8)
     sends.drain()
     assert sends.count <= SENDS
 

time: 134 us -> 129 us (0.963)
  Pallas kernels: 131 us -> 125 us
    pallas_call x1, Pallas kernels: 129 us -> 123 us  [local(): pl.pallas_call(kernel, out_shape=results, in_specs=[smem, vmem, hbm, vmem...]
where the time goes in v5:
time: 129 us; the launch traced here: 128 us
  Pallas kernels  125 us (97%)
  other arithmetic  2.16 us (2%)
    pallas_call x1, Pallas kernels, local(): pl.pallas_call(kernel, out_shape=results, in_specs=[smem, vmem, hbm, vmem...  123 us

profile of v5, /device:TPU:0, one launch (start us, length us, event | category | flops | bytes accessed | tf_op | source)
XLA Modules:
  0.0 128.2 jit_solution(5267335414290918333)
XLA Ops:
  0.6 0.7 multiply_add_fusion
  1.4 0.7 bitcast_select_fusion
  2.0 0.2 select_reduce_fusion
  2.2 0.6 broadcast_add_fusion.inv
  2.8 123.2 %graph_layer.1 = (bf16[512,256]{1,0:T(8,128)(2,1)}, f32[512,256]{1,0:T(8,128)}, f32[256,256]{1,0:T(8,128)}) custom-call(s32[32,64]{1,0:T(8,128)} %broadcast_add_fusion.inv, bf16[512,256]{1,0:T(8,128)(2,1)} %f_ref.1, bf16[384,128,128]{2,1,0:T(8,128)(2,1)} %bitcast.4, bf16[256,256]{1,0:T(8,128)(2,1)} %w_ref.1, bf16[512,256]{1,0:T(8,128)(2,1)} %ct_ref.1), custom_call_target="tpu_custom_call" | custom-call | tf_op jit(solution)/shard_map/graph_layer/pallas_call | solution.py:534
  126.0 2.2 %results.1 = (bf16[512,256]{1,0:T(8,128)(2,1)}, f32[512,256]{1,0:T(8,128)}, f32[256,256]{1,0:T(8,128)}) custom-call(bf16[512,256]{1,0:T(8,128)(2,1)} %get-tuple-element.9.refs_0_, f32[512,256]{1,0:T(8,128)} %get-tuple-element.10.refs_1_, f32[256,256]{1,0:T(8,128)} %get-tuple-element.11.refs_2_), custom_call_target="tpu_custom_call" | custom-call | tf_op jit(solution)/shard_map/results/pallas_call | solution.py:574
